TPU v7x, 512 devices: a whole 4x8x8 slice. The times are simulated.
512 devices in a mesh: line: 2 (over core), tile: 256 (over z, y, x).
Axes of the slice: x: 4, y: 8, z: 8, core: 2. Of those that a mesh axis runs over, the one named last changes fastest.
Arguments:
- field: float32 [2, 256, 32768], P(None, 'line', 'tile'), as said below
- saturation: float32 [256, 32768], P('line', 'tile'), may hold values from 0.025 to 1
- solid_mask: int32 [2, 32768], P('line', 'tile'), may hold values 0 or 1
Outputs:
- new_field: float32 [2, 256, 32768], P(None, 'line', 'tile')
Inputs may be any that keep to these rules, and one draw needn't show every extreme that they name: 2048 * field lies within -8 to 8.
All inputs are finite; a program needn't handle non-finite values. No bound on the sum of `solid_mask` on one device may be relied on, other than what follows from the above.
Results may differ from a plain program's by a relative error of at most 0.0005.
Values sent between devices are 32-bit elements; how exact they have to be, the bound alone decides.
No kernel may reach another device: no remote copies, remote signals or barrier semaphores. Data moves between devices by JAX's collectives and lax.ppermute only.
A program may use at most 64 MiB of HBM per device.

v0:
```python
import jax
import jax.numpy as jnp
from jax import lax
from jax.experimental import pallas as pl
from jax.experimental.pallas import tpu as pltpu
from jax.sharding import PartitionSpec as P

XS = 64
ZSTIFF = 2048
HALF = 0.5 * ZSTIFF
STEPS = 16
CHUNKS = 8
LANES = 128
TILE = (CHUNKS, LANES)
LIMIT = 12 * 1024 * 1024


def mat_mul(a, b):
    return (
        a[0] * b[0] + a[1] * b[2],
        a[0] * b[1] + a[1] * b[3],
        a[2] * b[0] + a[3] * b[2],
        a[2] * b[1] + a[3] * b[3],
    )


def mat_vec(a, v):
    return (a[0] * v[0] + a[1] * v[1], a[2] * v[0] + a[3] * v[1])


def add(*items):
    total = items[0]
    for item in items[1:]:
        total = tuple(x + y for x, y in zip(total, item))
    return total


def inverse(a):
    scale = 1.0 / (a[0] * a[3] - a[1] * a[2])
    return (a[3] * scale, -a[1] * scale, -a[2] * scale, a[0] * scale)


def full(k):
    return (k[0], 0.5 * k[2], 0.2 * k[2], k[1])


def conduct(signed):
    dry = jnp.maximum(signed, 0.0)
    moist = 0.004 + dry * dry * dry
    pore = signed > 0.0
    solid = signed < 0.0
    heat = jnp.where(pore, 1.0 + 2.0 * dry, jnp.where(solid, 3.0, 0.0))
    cross = jnp.where(pore, moist, 0.0)
    return (heat, jnp.where(solid, 0.004, cross), cross)


def flux(k, drop):
    return mat_vec(full(k), drop)


def roll(x, shift, axis):
    return pltpu.roll(x, shift % x.shape[axis], axis)


def down(items, shift):
    return tuple(roll(x, shift, 0) for x in items)


def lanes():
    return lax.broadcasted_iota(jnp.int32, TILE, 1)


def chunks():
    return lax.broadcasted_iota(jnp.int32, TILE, 0)


def toward_odd():
    parity = lax.rem(lax.axis_index("tile"), 2)
    return (lanes() >= XS) == (parity == 1)


def load(ref, *index):
    return tuple(ref[(*index, j)] for j in range(ref.shape[len(index)]))


def store(ref, index, items):
    for j, item in enumerate(items):
        ref[(*index, j)] = item


def levels():
    stride = 1
    while stride < STEPS:
        yield stride, range(0, STEPS, 2 * stride), range(stride, STEPS, 2 * stride)
        stride *= 2


def rows_of():
    place, at = {}, 0
    for stride, kept, _ in levels():
        for step in kept:
            place[stride, step] = at
            at += 1
    return place


PLACE = rows_of()


def prepare(field_hbm, sat_hbm, mask_hbm, field, signed, odd, even, fbuf, sbuf, mbuf, sems):
    copies = [
        pltpu.make_async_copy(mask_hbm, mbuf, sems.at[0]),
        pltpu.make_async_copy(sat_hbm, sbuf, sems.at[1]),
        pltpu.make_async_copy(field_hbm.at[0], fbuf.at[0], sems.at[2]),
        pltpu.make_async_copy(field_hbm.at[1], fbuf.at[1], sems.at[3]),
    ]
    for copy in copies:
        copy.start()
    for copy in copies:
        copy.wait()
    near = toward_odd()
    solid = jnp.broadcast_to(mbuf[...], TILE) > 0
    held = []
    for i in range(STEPS):
        here = pl.ds(i, CHUNKS, stride=STEPS)
        f0, f1, s = fbuf[0, here, :], fbuf[1, here, :], sbuf[here, :]
        s = jnp.where(solid, -s, s)
        field[0, i], field[1, i], signed[i] = f0, f1, s
        held.append(s)
        f1 = roll(f1, XS, 1)
        odd[i] = jnp.where(near, f0, f1)
        even[i] = jnp.where(near, f1, f0)
    for i in range(STEPS // 2):
        low, high = held[i], roll(held[i + STEPS // 2], XS, 1)
        odd[STEPS + i] = jnp.where(near, low, high)
        even[STEPS + i] = jnp.where(near, high, low)


def local(field, signed, k_all, rhs, ab, dpq, ring, final, answer, share):
    line = lax.axis_index("line")
    first, last = chunks() == 0, chunks() == CHUNKS - 1
    low_line, high_line = line == 0, line == 1
    column = lax.rem(lanes(), XS)
    west_end, east_end = column == 0, column == XS - 1
    zero = jnp.zeros(TILE, jnp.float32)
    one = jnp.ones(TILE, jnp.float32)
    unit = (one, zero, zero, one)

    k = []
    for i in range(STEPS):
        ki = conduct(signed[i])
        k.append(ki)
        store(k_all, (i,), ki)
        f = (field[0, i], field[1, i])
        both = (*ki, *f)
        other = tuple(roll(x, XS, 1) for x in both)
        total = flux(add(ki, other[:3]), (other[3] - f[0], other[4] - f[1]))
        before = tuple(jnp.where(west_end, 0.0, roll(x, 1, 1)) for x in both)
        west = flux(add(ki, before[:3]), (before[3] - f[0], before[4] - f[1]))
        edge = flux(ki, (-f[0], -f[1]))
        east = tuple(jnp.where(east_end, e, -roll(w, -1, 1)) for e, w in zip(edge, west))
        total = add(total, west, east)
        rhs[0, i] = f[0] + HALF * total[0]
        rhs[1, i] = f[1] + HALF * total[1]

    faces = [full(tuple(HALF * (x + y) for x, y in zip(k[i], k[i + 1]))) for i in range(STEPS - 1)]
    after = down(k[0], -1)
    outer = full(tuple(HALF * (x + y) for x, y in zip(k[-1], after)))
    faces.append(tuple(jnp.where(last, 0.0, x) for x in outer))
    entry = down(faces[-1], 1)
    bottom = jnp.logical_and(first, low_line)
    top = jnp.logical_and(last, high_line)
    excess = {i: unit for i in range(STEPS)}
    excess[0] = add(unit, tuple(jnp.where(bottom, HALF * x, 0.0) for x in full(k[0])))
    excess[STEPS - 1] = add(unit, tuple(jnp.where(top, HALF * x, 0.0) for x in full(k[-1])))
    lower = {i: faces[i - 1] if i else entry for i in range(STEPS)}
    upper = {i: faces[i] for i in range(STEPS)}

    for stride, kept, dropped in levels():
        inv = {}
        for i in dropped:
            inv[i] = inverse(add(excess[i], lower[i], upper[i]))
            store(dpq, (i,), (*inv[i], *mat_mul(inv[i], lower[i]), *mat_mul(inv[i], upper[i])))
        for i in kept:
            right = i + stride
            left = i - stride
            if left < 0:
                left += STEPS
                prev = tuple(down(x[left], 1) for x in (inv, lower, excess))
            else:
                prev = tuple(x[left] for x in (inv, lower, excess))
            a = mat_mul(lower[i], prev[0])
            b = mat_mul(upper[i], inv[right])
            store(ab, (PLACE[stride, i],), (*a, *b))
            up_a = a if prev[2] is unit else mat_mul(a, prev[2])
            up_b = b if excess[right] is unit else mat_mul(b, excess[right])
            excess[i] = add(excess[i], up_a, up_b)
            lower[i] = mat_mul(a, prev[1])
            upper[i] = mat_mul(b, upper[right])

    start = jnp.logical_and(high_line, first)
    end = jnp.logical_and(low_line, last)
    sides = {STEPS - 1: tuple(jnp.where(end, x, 0.0) for x in unit)}
    source = None
    for stride, kept, _ in levels():
        i = kept[-1]
        b = load(ab, PLACE[stride, i])[4:8]
        source = tuple(jnp.where(end, x, 0.0) for x in b) if source is None else mat_mul(b, source)
        sides[i] = source
    vec = add(tuple(jnp.where(start, x, 0.0) for x in unit), sides[0])

    low, up, ex = lower[0], upper[0], excess[0]
    shift, place = 1, 0
    while shift < CHUNKS:
        inv = inverse(add(ex, low, up))
        a = mat_mul(low, down(inv, shift))
        b = mat_mul(up, down(inv, -shift))
        store(ring, (place,), (*a, *b))
        vec = add(vec, mat_mul(a, down(vec, shift)), mat_mul(b, down(vec, -shift)))
        ex = add(ex, mat_mul(a, down(ex, shift)), mat_mul(b, down(ex, -shift)))
        low, up = mat_mul(a, down(low, shift)), mat_mul(b, down(up, -shift))
        shift *= 2
        place += 1
    inv = inverse(ex)
    store(final, (), inv)
    w = {0: mat_mul(inv, vec)}
    for stride, kept, dropped in reversed(list(levels())):
        for i in dropped:
            d = load(dpq, i)
            right = w[i + stride] if i + stride < STEPS else down(w[0], -1)
            w[i] = add(mat_mul(d[4:8], w[i - stride]), mat_mul(d[8:12], right))
            if i in sides:
                w[i] = add(w[i], mat_mul(d[0:4], sides[i]))
    for i in range(STEPS):
        store(answer, (i,), w[i])

    tail = (*down(w[STEPS - 1], 1), *down(k[STEPS - 1], 1))
    head = (*w[0], *k[0])
    for j, (x, y) in enumerate(zip(head, tail)):
        share[pl.ds(2 + j, 1), :] = jnp.where(low_line, y, x)[0:1]


def finish(field, k_all, rhs, ab, dpq, ring, final, share, odd, even, local_x, message):
    line = lax.axis_index("line")
    parity = lax.rem(lax.axis_index("tile"), 2)
    near = toward_odd()
    theirs = 1 - parity
    half = STEPS // 2
    far_signed = [None] * STEPS
    for i in range(half):
        o, e = odd[STEPS + i], even[theirs, STEPS + i]
        far_signed[i] = roll(jnp.where(near, e, o), XS, 1)
        far_signed[i + half] = jnp.where(near, o, e)
    b = {}
    for i in range(STEPS):
        o, e = odd[i], even[theirs, i]
        far = (roll(jnp.where(near, e, o), XS, 1), jnp.where(near, o, e))
        drop = (far[0] - field[0, i], far[1] - field[1, i])
        total = flux(add(load(k_all, i), conduct(far_signed[i])), drop)
        b[i] = (rhs[0, i] + HALF * total[0], rhs[1, i] + HALF * total[1])
    for stride, kept, _ in levels():
        for i in kept:
            left = i - stride
            prev = b[left] if left >= 0 else down(b[left + STEPS], 1)
            c = load(ab, PLACE[stride, i])
            b[i] = add(b[i], mat_vec(c[0:4], prev), mat_vec(c[4:8], b[i + stride]))
    vec = b[0]
    shift, place = 1, 0
    while shift < CHUNKS:
        c = load(ring, place)
        vec = add(vec, mat_vec(c[0:4], down(vec, shift)), mat_vec(c[4:8], down(vec, -shift)))
        shift *= 2
        place += 1
    x = {0: mat_vec(load(final), vec)}
    for stride, _, dropped in reversed(list(levels())):
        for i in dropped:
            d = load(dpq, i)
            right = x[i + stride] if i + stride < STEPS else down(x[0], -1)
            x[i] = add(mat_vec(d[0:4], b[i]), mat_vec(d[4:8], x[i - stride]), mat_vec(d[8:12], right))
    for i in range(STEPS):
        store(local_x, (i,), x[i])
    message[...] = share[...]
    tail = down(x[STEPS - 1], 1)
    for j in range(2):
        message[pl.ds(j, 1), :] = jnp.where(line == 0, tail[j], x[0][j])[0:1]


def join(local_x, answer, both, out):
    line = lax.axis_index("line")

    def row(who, j):
        return jnp.broadcast_to(both[who, pl.ds(j, 1), :], TILE)

    sign = jnp.where(line == 0, 1.0, -1.0)
    drop = tuple(sign * (row(1, j) - row(0, j)) for j in range(2))
    reach = tuple(row(0, 2 + j) + row(1, 2 + j) for j in range(4))
    face = full(tuple(HALF * (row(0, 6 + j) + row(1, 6 + j)) for j in range(3)))
    one, zero = jnp.ones(TILE, jnp.float32), jnp.zeros(TILE, jnp.float32)
    inv = inverse(add((one, zero, zero, one), mat_mul(face, reach)))
    through = mat_vec(inv, mat_vec(face, drop))
    for i in range(STEPS):
        x = add(load(local_x, i), mat_vec(load(answer, i), through))
        here = pl.ds(i, CHUNKS, stride=STEPS)
        out[0, here, :] = x[0]
        out[1, here, :] = x[1]


def tiles(*lead):
    return jax.ShapeDtypeStruct((*lead, *TILE), jnp.float32)


def call(kernel, outs, args, name, flops, **more):
    vmem = pl.BlockSpec(memory_space=pltpu.VMEM)
    more.setdefault("in_specs", [vmem] * len(args))
    one = not isinstance(outs, (list, tuple))
    return pl.pallas_call(
        kernel,
        out_shape=outs,
        out_specs=vmem if one else [vmem] * len(outs),
        compiler_params=pltpu.CompilerParams(vmem_limit_bytes=LIMIT),
        cost_estimate=pl.CostEstimate(flops=flops, bytes_accessed=1 << 20, transcendentals=0),
        name=name,
        **more,
    )(*args)


def body(field, saturation, solid_mask):
    count = lax.axis_size("tile")
    evens = [[t, t + 1] for t in range(0, count, 2)]
    odds = [pair for t in range(1, count - 1, 2) for pair in ((t, t + 1), (t + 1, t))]
    cells = STEPS * CHUNKS
    pack = STEPS + STEPS // 2
    kept, signed, odd, even = call(
        prepare,
        [tiles(2, STEPS), tiles(STEPS), tiles(pack), tiles(pack)],
        (field, saturation, solid_mask),
        "prepare",
        1 << 16,
        in_specs=[pl.BlockSpec(memory_space=pl.ANY)] * 3,
        scratch_shapes=[
            pltpu.VMEM((2, cells, LANES), jnp.float32),
            pltpu.VMEM((cells, LANES), jnp.float32),
            pltpu.VMEM((1, LANES), jnp.int32),
            pltpu.SemaphoreType.DMA((4,)),
        ],
    )
    odd = lax.ppermute(odd, "tile", odds)
    even = lax.all_gather(even, "tile", axis_index_groups=evens, axis=0)
    k_all, rhs, ab, dpq, ring, final, answer, share = call(
        local,
        [
            tiles(STEPS, 3),
            tiles(2, STEPS),
            tiles(STEPS - 1, 8),
            tiles(STEPS, 12),
            tiles(3, 8),
            tiles(4),
            tiles(STEPS, 4),
            jax.ShapeDtypeStruct((16, LANES), jnp.float32),
        ],
        (kept, signed),
        "local",
        1 << 23,
    )
    local_x, message = call(
        finish,
        [tiles(STEPS, 2), jax.ShapeDtypeStruct((16, LANES), jnp.float32)],
        (kept, k_all, rhs, ab, dpq, ring, final, share, odd, even),
        "finish",
        1 << 21,
    )
    both = lax.all_gather(message, "line", axis=0)
    out = jax.ShapeDtypeStruct((2, cells, LANES), jnp.float32)
    return call(join, out, (local_x, answer, both), "join", 1 << 18)


def solution(mesh):
    in_specs = (P(None, "line", "tile"), P("line", "tile"), P("line", "tile"))
    out_specs = P(None, "line", "tile")
    return jax.shard_map(body, mesh=mesh, in_specs=in_specs, out_specs=out_specs, check_vma=False)
```

profile of v0, /device:TPU:449, one launch (start us, length us, event | category | flops | bytes accessed | tf_op | source)
XLA Modules:
  0.0 19.5 jit_solution(122999220862643731)
XLA Ops:
  0.0 0.0 copy-start
  0.0 0.9 %copy-done = f32[2,128,128]{2,1,0:T(8,128)S(1)} copy-done((f32[2,128,128]{2,1,0:T(8,128)S(1)}, f32[2,128,128]{2,1,0:T(8,128)}, u32[]{:S(2)}) %copy-start) | copy-done | bytes 131096
  0.9 0.0 copy-start.1
  0.9 0.8 %copy-done.1 = f32[128,128]{1,0:T(8,128)S(1)} copy-done((f32[128,128]{1,0:T(8,128)S(1)}, f32[128,128]{1,0:T(8,128)}, u32[]{:S(2)}) %copy-start.1) | copy-done | bytes 65560
  1.7 0.0 copy-start.2
  1.7 0.7 %copy-done.2 = s32[1,128]{1,0:T(1,128)S(1)} copy-done((s32[1,128]{1,0:T(1,128)S(1)}, s32[1,128]{1,0:T(1,128)}, u32[]{:S(2)}) %copy-start.2) | copy-done | bytes 536
  2.4 0.4 %prepare.1 = (f32[2,16,8,128]{3,2,1,0:T(8,128)S(1)}, f32[16,8,128]{2,1,0:T(8,128)S(1)}, f32[24,8,128]{2,1,0:T(8,128)S(1)}, f32[24,8,128]{2,1,0:T(8,128)S(1)}) custom-call(f32[2,128,128]{2,1,0:T(8,128)S(1)} %copy-done, f32[128,128]{1,0:T(8,128)S(1)} %copy-done.1, s32[1,128]{1,0:T(1,128)S(1)} %copy-done.2), custom_call_target="tpu_custom_call" | custom-call | flops 65536 | bytes 1048576 | tf_op jit(solution)/shard_map/prepare/pallas_call | solution.py:316
  2.8 7.3 %collective-permute-start = (f32[24,8,128]{2,1,0:T(8,128)S(1)}, f32[24,8,128]{2,1,0:T(8,128)S(1)}, u32[]{:S(2)}, u32[]{:S(2)}) collective-permute-start(f32[24,8,128]{2,1,0:T(8,128)S(1)} %get-tuple-element.28), channel_id=1, source_target_pairs={{1,2},{2,1},{3,4},{4,3},{5,6},{6,5},{7,8},{8,7},{9,10},{10,9},{11,... | collective-permute-start | bytes 294920 | tf_op jit(solution)/shard_map/ppermute | solution.py:347
  10.1 0.8 %local.1 = (f32[16,3,8,128]{3,2,1,0:T(8,128)S(1)}, f32[2,16,8,128]{3,2,1,0:T(8,128)S(1)}, f32[15,8,8,128]{3,2,1,0:T(8,128)S(1)}, f32[16,12,8,128]{3,2,1,0:T(8,12...) custom-call(f32[2,16,8,128]{3,2,1,0:T(8,128)S(1)} %get-tuple-element, ...), custom_call_target="tpu_custom_call" | custom-call | flops 8388608 | bytes 1048576 | tf_op jit(solution)/shard_map/local/pallas_call | solution.py:316
  10.8 4.1 %all-gather = f32[48,8,128]{2,1,0:T(8,128)S(1)} all-gather(f32[24,8,128]{2,1,0:T(8,128)S(1)} %get-tuple-element.29), channel_id=2, replica_groups={{0,1},{2,3},{4,5},{6,7},{8,9},{10,11},{12,13},{14,15},{16,17},{18,19},{..., dimensions={0}, use_global_device_ids=true | all-gather | bytes 294912 | tf_op jit(solution)/shard_map/all_gather | solution.py:348
  15.0 0.0 collective-permute-done.odd
  15.0 0.2 %finish.1 = (f32[16,2,8,128]{3,2,1,0:T(8,128)S(1)}, f32[16,128]{1,0:T(8,128)S(1)}) custom-call(f32[2,16,8,128]{3,2,1,0:T(8,128)S(1)} %get-tuple-element.19.field, f32[16,3,8,128]{3,2,1,0:T(8,128)S(1)} %get-tuple-element.21.k_all, f32[2,16,8,128]{3,2,1,0:T(8,128)S(1)} %get-tuple-element.22.rhs, f32[15,8,8,128]{3,2,1,0:T(8,128)S(1)} %get-tuple-element.23.ab, ...), custom_call_target="tpu_custom_call" | custom-call | flops 2097152 | bytes 1048576 | tf_op jit(solution)/shard_map/finish/pallas_call | solution.py:316
  15.2 3.6 %all-gather.1 = f32[32,128]{1,0:T(8,128)S(1)} all-gather(f32[16,128]{1,0:T(8,128)S(1)} %get-tuple-element.32), channel_id=3, replica_groups=mesh['line'=2,'tile'=256] {'line'}, dimensions={0}, use_global_device_ids=true | all-gather | bytes 24576 | tf_op jit(solution)/shard_map/all_gather | solution.py:372
  18.8 0.7 %join.1 = f32[2,128,128]{2,1,0:T(8,128)} custom-call(f32[16,2,8,128]{3,2,1,0:T(8,128)S(1)} %get-tuple-element.30.local_x, f32[16,4,8,128]{3,2,1,0:T(8,128)S(1)} %get-tuple-element.31.answer, f32[2,16,128]{2,1,0:T(8,128)S(1)} %bitcast.3), custom_call_target="tpu_custom_call" | custom-call | flops 262144 | bytes 1048576 | tf_op jit(solution)/shard_map/join/pallas_call | solution.py:316
Async XLA Ops:
  0.0 0.9 %copy-start = (f32[2,128,128]{2,1,0:T(8,128)S(1)}, f32[2,128,128]{2,1,0:T(8,128)}, u32[]{:S(2)}) copy-start(f32[2,128,128]{2,1,0:T(8,128)} %field_hbm.1) | copy-start | bytes 393220
  0.9 0.8 %copy-start.1 = (f32[128,128]{1,0:T(8,128)S(1)}, f32[128,128]{1,0:T(8,128)}, u32[]{:S(2)}) copy-start(f32[128,128]{1,0:T(8,128)} %sat_hbm.1) | copy-start | bytes 196612
  1.7 0.7 %copy-start.2 = (s32[1,128]{1,0:T(1,128)S(1)}, s32[1,128]{1,0:T(1,128)}, u32[]{:S(2)}) copy-start(s32[1,128]{1,0:T(1,128)} %mask_hbm.1) | copy-start | bytes 1540
  2.8 12.2 %collective-permute-start = (f32[24,8,128]{2,1,0:T(8,128)S(1)}, f32[24,8,128]{2,1,0:T(8,128)S(1)}, u32[]{:S(2)}, u32[]{:S(2)}) collective-permute-start(f32[24,8,128]{2,1,0:T(8,128)S(1)} %get-tuple-element.28), channel_id=1, source_target_pairs={{1,2},{2,1},{3,4},{4,3},{5,6},{6,5},{7,8},{8,7},{9,10},{10,9},{11,... | collective-permute-start | bytes 294920 | tf_op jit(solution)/shard_map/ppermute | solution.py:347
where the time goes:
time: 19.7 us; the launch traced here: 19.5 us
  blocking collectives  7.74 us (39%)
  starting transfers between devices  7.28 us (37%)
  local copies, waits for them, and re-layouts  2.4 us (12%)
  Pallas kernels  2.08 us (11%)
    ppermute x1, starting transfers between devices, body(): odd = lax.ppermute(odd, 'tile', odds)  7.28 us
    all_gather x1, blocking collectives, body(): even = lax.all_gather(even, 'tile', axis_index_groups=evens, axis=0)  4.14 us
    all_gather x1, blocking collectives, body(): both = lax.all_gather(message, 'line', axis=0)  3.6 us
    unnamed x6, local copies, waits for them, and re-layouts  2.4 us
    pallas_call x4, Pallas kernels, call(): pl.pallas_call(kernel, out_shape=outs, out_specs=vmem if one else [vmem]...  2.08 us
  transfers between devices with their start and end apart: 1, of which 0 were waited for; matrix products, arithmetic and copies ran while one was open for 0% of the time, Pallas kernels for 4%

commit v1 on v0

--- a/solution.py
+++ b/solution.py
@@ -330,13 +330,14 @@
     odds = [pair for t in range(1, count - 1, 2) for pair in ((t, t + 1), (t + 1, t))]
     cells = STEPS * CHUNKS
     pack = STEPS + STEPS // 2
+    args = [pltpu.with_memory_space_constraint(x, pltpu.HBM) for x in (field, saturation, solid_mask)]
     kept, signed, odd, even = call(
         prepare,
         [tiles(2, STEPS), tiles(STEPS), tiles(pack), tiles(pack)],
-        (field, saturation, solid_mask),
+        args,
         "prepare",
         1 << 16,
-        in_specs=[pl.BlockSpec(memory_space=pl.ANY)] * 3,
+        in_specs=[pl.BlockSpec(memory_space=pltpu.HBM)] * 3,
         scratch_shapes=[
             pltpu.VMEM((2, cells, LANES), jnp.float32),
             pltpu.VMEM((cells, LANES), jnp.float32),

time: 19.7 us -> 18 us (0.914)
  local copies, waits for them, and re-layouts: 2.4 us -> 0 us
  Pallas kernels: 2.08 us -> 2.76 us
    unnamed x6 -> x0, local copies, waits for them, and re-layouts: 2.4 us -> none
    pallas_call x4, Pallas kernels: 2.08 us -> 2.76 us  [call(): pl.pallas_call(kernel, out_shape=outs, out_specs=vmem if one else [vmem]...]
where the time goes in v1:
time: 18 us; the launch traced here: 17.8 us
  blocking collectives  7.74 us (43%)
  starting transfers between devices  7.28 us (40%)
  Pallas kernels  2.76 us (15%)
    ppermute x1, starting transfers between devices, body(): odd = lax.ppermute(odd, 'tile', odds)  7.28 us
    all_gather x1, blocking collectives, body(): even = lax.all_gather(even, 'tile', axis_index_groups=evens, axis=0)  4.14 us
    all_gather x1, blocking collectives, body(): both = lax.all_gather(message, 'line', axis=0)  3.6 us
    pallas_call x4, Pallas kernels, call(): pl.pallas_call(kernel, out_shape=outs, out_specs=vmem if one else [vmem]...  2.76 us
  transfers between devices with their start and end apart: 1, of which 0 were waited for; matrix products, arithmetic and copies ran while one was open for 0% of the time, Pallas kernels for 4%

profile of v1, /device:TPU:449, one launch (start us, length us, event | category | flops | bytes accessed | tf_op | source)
XLA Modules:
  0.0 17.8 jit_solution(159193523920056321)
XLA Ops:
  0.0 1.1 %prepare.1 = (f32[2,16,8,128]{3,2,1,0:T(8,128)S(1)}, f32[16,8,128]{2,1,0:T(8,128)S(1)}, f32[24,8,128]{2,1,0:T(8,128)S(1)}, f32[24,8,128]{2,1,0:T(8,128)S(1)}) custom-call(f32[2,128,128]{2,1,0:T(8,128)} %field_hbm.1, f32[128,128]{1,0:T(8,128)} %sat_hbm.1, s32[1,128]{1,0:T(1,128)} %mask_hbm.1), custom_call_target="tpu_custom_call" | custom-call | flops 65536 | bytes 1048576 | tf_op jit(solution)/shard_map/prepare/pallas_call | solution.py:316
  1.1 7.3 %collective-permute-start = (f32[24,8,128]{2,1,0:T(8,128)S(1)}, f32[24,8,128]{2,1,0:T(8,128)S(1)}, u32[]{:S(2)}, u32[]{:S(2)}) collective-permute-start(f32[24,8,128]{2,1,0:T(8,128)S(1)} %get-tuple-element.28), channel_id=1, source_target_pairs={{1,2},{2,1},{3,4},{4,3},{5,6},{6,5},{7,8},{8,7},{9,10},{10,9},{11,... | collective-permute-start | bytes 294920 | tf_op jit(solution)/shard_map/ppermute | solution.py:348
  8.4 0.8 %local.1 = (f32[16,3,8,128]{3,2,1,0:T(8,128)S(1)}, f32[2,16,8,128]{3,2,1,0:T(8,128)S(1)}, f32[15,8,8,128]{3,2,1,0:T(8,128)S(1)}, f32[16,12,8,128]{3,2,1,0:T(8,12...) custom-call(f32[2,16,8,128]{3,2,1,0:T(8,128)S(1)} %get-tuple-element, ...), custom_call_target="tpu_custom_call" | custom-call | flops 8388608 | bytes 1048576 | tf_op jit(solution)/shard_map/local/pallas_call | solution.py:316
  9.1 4.1 %all-gather = f32[48,8,128]{2,1,0:T(8,128)S(1)} all-gather(f32[24,8,128]{2,1,0:T(8,128)S(1)} %get-tuple-element.29), channel_id=2, replica_groups={{0,1},{2,3},{4,5},{6,7},{8,9},{10,11},{12,13},{14,15},{16,17},{18,19},{..., dimensions={0}, use_global_device_ids=true | all-gather | bytes 294912 | tf_op jit(solution)/shard_map/all_gather | solution.py:349
  13.3 0.0 collective-permute-done.odd
  13.3 0.2 %finish.1 = (f32[16,2,8,128]{3,2,1,0:T(8,128)S(1)}, f32[16,128]{1,0:T(8,128)S(1)}) custom-call(f32[2,16,8,128]{3,2,1,0:T(8,128)S(1)} %get-tuple-element.19.field, f32[16,3,8,128]{3,2,1,0:T(8,128)S(1)} %get-tuple-element.21.k_all, f32[2,16,8,128]{3,2,1,0:T(8,128)S(1)} %get-tuple-element.22.rhs, f32[15,8,8,128]{3,2,1,0:T(8,128)S(1)} %get-tuple-element.23.ab, ...), custom_call_target="tpu_custom_call" | custom-call | flops 2097152 | bytes 1048576 | tf_op jit(solution)/shard_map/finish/pallas_call | solution.py:316
  13.5 3.6 %all-gather.1 = f32[32,128]{1,0:T(8,128)S(1)} all-gather(f32[16,128]{1,0:T(8,128)S(1)} %get-tuple-element.32), channel_id=3, replica_groups=mesh['line'=2,'tile'=256] {'line'}, dimensions={0}, use_global_device_ids=true | all-gather | bytes 24576 | tf_op jit(solution)/shard_map/all_gather | solution.py:373
  17.1 0.7 %join.1 = f32[2,128,128]{2,1,0:T(8,128)} custom-call(f32[16,2,8,128]{3,2,1,0:T(8,128)S(1)} %get-tuple-element.30.local_x, f32[16,4,8,128]{3,2,1,0:T(8,128)S(1)} %get-tuple-element.31.answer, f32[2,16,128]{2,1,0:T(8,128)S(1)} %bitcast.3), custom_call_target="tpu_custom_call" | custom-call | flops 262144 | bytes 1048576 | tf_op jit(solution)/shard_map/join/pallas_call | solution.py:316
Async XLA Ops:
  1.1 12.2 %collective-permute-start = (f32[24,8,128]{2,1,0:T(8,128)S(1)}, f32[24,8,128]{2,1,0:T(8,128)S(1)}, u32[]{:S(2)}, u32[]{:S(2)}) collective-permute-start(f32[24,8,128]{2,1,0:T(8,128)S(1)} %get-tuple-element.28), channel_id=1, source_target_pairs={{1,2},{2,1},{3,4},{4,3},{5,6},{6,5},{7,8},{8,7},{9,10},{10,9},{11,... | collective-permute-start | bytes 294920 | tf_op jit(solution)/shard_map/ppermute | solution.py:348

commit v2 on v1

v2 whole, which is shorter than its diff:
```python
import jax
import jax.numpy as jnp
from jax import lax
from jax.experimental import pallas as pl
from jax.experimental.pallas import tpu as pltpu
from jax.sharding import PartitionSpec as P

XS = 64
ZSTIFF = 2048
HALF = 0.5 * ZSTIFF
STEPS = 16
CHUNKS = 8
LANES = 128
TILE = (CHUNKS, LANES)
ROW = 4
SCALE = 0.4**0.5
CROSS = 0.1**0.5
LIMIT = 12 * 1024 * 1024


def mul(a, b):
    return (
        a[0] * b[0] + a[1] * b[2],
        a[0] * b[1] + a[1] * b[3],
        a[2] * b[0] + a[3] * b[2],
        a[2] * b[1] + a[3] * b[3],
    )


def wide(s):
    return (s[0], s[1], s[1], s[2])


def turn(a):
    return (a[0], a[2], a[1], a[3])


def apply(a, v):
    return (a[0] * v[0] + a[1] * v[1], a[2] * v[0] + a[3] * v[1])


def add(*items):
    total = items[0]
    for item in items[1:]:
        total = tuple(x + y for x, y in zip(total, item))
    return total


def symmetric(a, *more):
    return add(*((m[0], m[1], m[3]) for m in (a, *more)))


def inverse(s):
    scale = 1.0 / (s[0] * s[2] - s[1] * s[1])
    return (s[2] * scale, -s[1] * scale, s[0] * scale)


def conduct(signed):
    dry = jnp.maximum(signed, 0.0)
    moist = 0.004 + dry * dry * dry
    pore = signed > 0.0
    return (jnp.where(pore, 1.0 + 2.0 * signed, 3.0), jnp.where(pore, CROSS * moist, 0.0), moist)


def conduct_or_none(signed):
    inside = signed != 0.0
    heat, cross, moist = conduct(signed)
    return (jnp.where(inside, heat, 0.0), cross, jnp.where(inside, moist, 0.0))


def flux(k, drop):
    return (k[0] * drop[0] + k[1] * drop[1], k[1] * drop[0] + k[2] * drop[1])


def roll(x, shift, axis):
    return pltpu.roll(x, shift % x.shape[axis], axis)


def down(items, shift):
    return tuple(roll(x, shift, 0) for x in items)


def lanes():
    return lax.broadcasted_iota(jnp.int32, TILE, 1)


def chunks():
    return lax.broadcasted_iota(jnp.int32, TILE, 0)


def toward_odd():
    parity = lax.rem(lax.axis_index("tile"), 2)
    return (lanes() >= XS) == (parity == 1)


def load(ref, *index):
    return tuple(ref[(*index, j)] for j in range(ref.shape[len(index)]))


def store(ref, index, items):
    for j, item in enumerate(items):
        ref[(*index, j)] = item


def levels():
    stride = 1
    while stride < STEPS:
        yield stride, range(0, STEPS, 2 * stride), range(stride, STEPS, 2 * stride)
        stride *= 2


def rows_of():
    place, at = {}, 0
    for stride, kept, _ in levels():
        for step in kept:
            place[stride, step] = at
            at += 1
    return place


PLACE = rows_of()


def prepare(field_hbm, sat_hbm, mask_hbm, kept, turned, odd, fbuf, sbuf, mbuf, sems):
    fetch_f1 = pltpu.make_async_copy(field_hbm.at[1], fbuf.at[1], sems.at[0])
    fetch_s = pltpu.make_async_copy(sat_hbm, sbuf, sems.at[1])
    fetch_mask = pltpu.make_async_copy(mask_hbm, mbuf, sems.at[2])
    fetch_f0 = pltpu.make_async_copy(field_hbm.at[0], fbuf.at[0], sems.at[3])
    for copy in (fetch_f1, fetch_s, fetch_mask, fetch_f0):
        copy.start()
    near = toward_odd()
    half = STEPS // 2
    rows = [pl.ds(i, CHUNKS, stride=STEPS) for i in range(STEPS)]
    fetch_f1.wait()
    for i in range(STEPS):
        f1 = fbuf[1, rows[i], :] * (1.0 / SCALE)
        kept[1, i] = f1
        turned[i] = roll(f1, XS, 1)
    fetch_s.wait()
    fetch_mask.wait()
    solid = jnp.broadcast_to(mbuf[...], TILE) > 0
    for i in range(STEPS):
        s = sbuf[rows[i], :]
        s = jnp.where(solid, -s, s)
        kept[2, i] = s
        if i >= half:
            high = roll(s, XS, 1)
            turned[STEPS + i - half] = high
            odd[STEPS + i - half] = jnp.where(near, kept[2, i - half], high)
    fetch_f0.wait()
    for i in range(STEPS):
        f0 = fbuf[0, rows[i], :]
        kept[0, i] = f0
        odd[i] = jnp.where(near, f0, turned[i])


def waits_long():
    return lax.rem(lax.axis_index("tile"), ROW) == 0


def early(field_hbm, sat_hbm, mask_hbm, kept, turned, odd, *rest):
    prepare(field_hbm, sat_hbm, mask_hbm, kept, turned, odd, *rest[-4:])

    @pl.when(waits_long())
    def _():
        local(kept, turned, *rest[:-4])


def late(kept, turned, *rest):
    @pl.when(jnp.logical_not(waits_long()))
    def _():
        local(kept, turned, *rest[len(rest) // 2 :])


def local(kept, turned, even, k_all, rhs, ab, dinv, ring, final, answer, share):
    line = lax.axis_index("line")
    first, last = chunks() == 0, chunks() == CHUNKS - 1
    low_line, high_line = line == 0, line == 1
    near = toward_odd()
    column = lax.rem(lanes(), XS)
    west_end, east_end = column == 0, column == XS - 1
    zero = jnp.zeros(TILE, jnp.float32)
    one = jnp.ones(TILE, jnp.float32)
    unit = (one, zero, zero, one)
    half = STEPS // 2

    for i in range(STEPS):
        even[i] = jnp.where(near, turned[i], kept[0, i])
    for i in range(half):
        even[STEPS + i] = jnp.where(near, turned[STEPS + i], kept[2, i])

    k = []
    for i in range(STEPS):
        s = kept[2, i]
        ki = conduct(s)
        k.append(ki)
        store(k_all, (i,), ki)
        f = (kept[0, i], kept[1, i])
        far = (roll(f[0], XS, 1), turned[i])
        far_s = turned[STEPS + i - half] if i >= half else roll(s, XS, 1)
        total = flux(add(ki, conduct(far_s)), (far[0] - f[0], far[1] - f[1]))
        west_k = conduct(roll(s, 1, 1))
        west = flux(add(ki, west_k), (roll(f[0], 1, 1) - f[0], roll(f[1], 1, 1) - f[1]))
        edge = flux(ki, f)
        west = tuple(jnp.where(west_end, -e, w) for e, w in zip(edge, west))
        east = tuple(jnp.where(east_end, e, roll(w, -1, 1)) for e, w in zip(edge, west))
        for j in range(2):
            rhs[j, i] = f[j] + HALF * (total[j] + (west[j] - east[j]))

    upper = {i: wide(tuple(HALF * (x + y) for x, y in zip(k[i], k[i + 1]))) for i in range(STEPS - 1)}
    outer = tuple(HALF * (x + y) for x, y in zip(k[-1], down(k[0], -1)))
    upper[STEPS - 1] = wide(tuple(jnp.where(last, 0.0, x) for x in outer))
    bottom = jnp.logical_and(first, low_line)
    top = jnp.logical_and(last, high_line)
    bottom = wide(tuple(jnp.where(bottom, HALF * x, 0.0) for x in k[0]))
    top = wide(tuple(jnp.where(top, HALF * x, 0.0) for x in k[-1]))
    excess = {i: unit for i in range(STEPS)}
    excess[0] = add(unit, bottom)
    excess[STEPS - 1] = add(unit, top)

    for stride, keep, drop in levels():
        lower = {}
        for i in (*keep, *drop):
            left = i - stride
            lower[i] = turn(upper[left] if left >= 0 else down(upper[left + STEPS], 1))
        inv = {}
        for i in drop:
            inv[i] = inverse(symmetric(excess[i], lower[i], upper[i]))
            store(dinv, (i,), inv[i])
        for i in keep:
            right, left = i + stride, i - stride
            if left < 0:
                before = wide(down(inv[left + STEPS], 1))
            else:
                before = wide(inv[left])
            a = mul(lower[i], before)
            b = mul(upper[i], wide(inv[right]))
            store(ab, (PLACE[stride, i],), (*a, *b))
            if stride == 1:
                more = add(excess[i], a, b)
                if right == STEPS - 1:
                    more = add(more, mul(b, top))
            else:
                prev = excess[left] if left >= 0 else down(excess[left + STEPS], 1)
                more = add(excess[i], mul(a, prev), mul(b, excess[right]))
            excess[i] = more
            upper[i] = mul(b, upper[right])

    start = jnp.logical_and(high_line, first)
    end = jnp.logical_and(low_line, last)
    sides = {STEPS - 1: tuple(jnp.where(end, x, 0.0) for x in unit)}
    source = None
    for stride, keep, _ in levels():
        i = keep[-1]
        b = load(ab, PLACE[stride, i])[4:8]
        source = tuple(jnp.where(end, x, 0.0) for x in b) if source is None else mul(b, source)
        sides[i] = source
    vec = add(tuple(jnp.where(start, x, 0.0) for x in unit), sides[0])

    up, ex = upper[0], excess[0]
    low = turn(down(up, 1))
    shift, place = 1, 0
    while shift < CHUNKS:
        inv = inverse(symmetric(ex, low, up))
        a = mul(low, wide(down(inv, shift)))
        b = mul(up, wide(down(inv, -shift)))
        store(ring, (place,), (*a, *b))
        vec = add(vec, mul(a, down(vec, shift)), mul(b, down(vec, -shift)))
        ex = add(ex, mul(a, down(ex, shift)), mul(b, down(ex, -shift)))
        up = mul(b, down(up, -shift))
        shift *= 2
        place += 1
        low = turn(down(up, shift))
    inv = inverse(symmetric(ex))
    store(final, (), inv)
    w = {0: mul(wide(inv), vec)}
    for stride, keep, drop in reversed(list(levels())):
        for i in drop:
            left, right = i - stride, i + stride
            prev = turn(load(ab, PLACE[stride, left])[4:8])
            if right < STEPS:
                after, later = turn(load(ab, PLACE[stride, right])[0:4]), w[right]
            else:
                after, later = turn(down(load(ab, PLACE[stride, 0])[0:4], -1)), down(w[0], -1)
            w[i] = add(mul(prev, w[left]), mul(after, later))
            if i in sides:
                w[i] = add(w[i], mul(wide(load(dinv, i)), sides[i]))
    for i in range(STEPS):
        store(answer, (i,), (w[i][0], w[i][1], SCALE * w[i][2], SCALE * w[i][3]))

    tail = w[STEPS - 1]
    tail = down((tail[0], tail[1], tail[3], kept[2, STEPS - 1]), 1)
    head = (w[0][0], w[0][1], w[0][3], kept[2, 0])
    for j, (x, y) in enumerate(zip(head, tail)):
        share[pl.ds(2 + j, 1), :] = jnp.where(low_line, y, x)[0:1]
    share[pl.ds(0, 2), :] = zero[0:2]
    share[pl.ds(6, 2), :] = zero[0:2]


def finish(k_all, rhs, kept, ab, dinv, ring, final, share, odd, even, local_x, message):
    line = lax.axis_index("line")
    theirs = 1 - lax.rem(lax.axis_index("tile"), 2)
    near = toward_odd()
    half = STEPS // 2
    far_signed = [None] * STEPS
    for i in range(half):
        o, e = odd[STEPS + i], even[theirs, STEPS + i]
        far_signed[i] = roll(jnp.where(near, e, o), XS, 1)
        far_signed[i + half] = jnp.where(near, o, e)
    b = {}
    for i in range(STEPS):
        o, e = odd[i], even[theirs, i]
        far = (roll(jnp.where(near, e, o), XS, 1), jnp.where(near, o, e))
        drop = (far[0] - kept[0, i], far[1] - kept[1, i])
        total = flux(add(load(k_all, i), conduct_or_none(far_signed[i])), drop)
        b[i] = (rhs[0, i] + HALF * total[0], rhs[1, i] + HALF * total[1])
    for stride, keep, _ in levels():
        for i in keep:
            left = i - stride
            prev = b[left] if left >= 0 else down(b[left + STEPS], 1)
            c = load(ab, PLACE[stride, i])
            b[i] = add(b[i], apply(c[0:4], prev), apply(c[4:8], b[i + stride]))
    vec = b[0]
    shift, place = 1, 0
    while shift < CHUNKS:
        c = load(ring, place)
        vec = add(vec, apply(c[0:4], down(vec, shift)), apply(c[4:8], down(vec, -shift)))
        shift *= 2
        place += 1
    x = {0: apply(wide(load(final)), vec)}
    for stride, keep, drop in reversed(list(levels())):
        for i in drop:
            left, right = i - stride, i + stride
            prev = turn(load(ab, PLACE[stride, left])[4:8])
            if right < STEPS:
                after, later = turn(load(ab, PLACE[stride, right])[0:4]), x[right]
            else:
                after, later = turn(down(load(ab, PLACE[stride, 0])[0:4], -1)), down(x[0], -1)
            x[i] = add(apply(wide(load(dinv, i)), b[i]), apply(prev, x[left]), apply(after, later))
    for i in range(STEPS):
        store(local_x, (i,), (x[i][0], SCALE * x[i][1]))
    message[...] = share[...]
    tail = down(x[STEPS - 1], 1)
    for j in range(2):
        message[pl.ds(j, 1), :] = jnp.where(line == 0, tail[j], x[0][j])[0:1]


def join(local_x, answer, both, out_hbm, out, sems):
    line = lax.axis_index("line")

    def row(who, j):
        return jnp.broadcast_to(both[who, pl.ds(j, 1), :], TILE)

    sign = jnp.where(line == 0, 1.0, -1.0)
    drop = tuple(sign * (row(1, j) - row(0, j)) for j in range(2))
    reach = wide(tuple(row(0, 2 + j) + row(1, 2 + j) for j in range(3)))
    face = tuple(HALF * (x + y) for x, y in zip(conduct(row(0, 5)), conduct(row(1, 5))))
    m = mul(wide(face), reach)
    m = (m[0] + 1.0, m[1], m[2], m[3] + 1.0)
    push = flux(face, drop)
    scale = 1.0 / (m[0] * m[3] - m[1] * m[2])
    through = ((m[3] * push[0] - m[1] * push[1]) * scale, (m[0] * push[1] - m[2] * push[0]) * scale)
    copies = [pltpu.make_async_copy(out.at[j], out_hbm.at[j], sems.at[j]) for j in range(2)]
    for j in range(2):
        for i in range(STEPS):
            x = local_x[i, j] + (answer[i, 2 * j] * through[0] + answer[i, 2 * j + 1] * through[1])
            out[j, pl.ds(i, CHUNKS, stride=STEPS), :] = x
        copies[j].start()
    for copy in copies:
        copy.wait()


def tiles(*lead):
    return jax.ShapeDtypeStruct((*lead, *TILE), jnp.float32)


def call(kernel, outs, args, name, flops, **more):
    vmem = pl.BlockSpec(memory_space=pltpu.VMEM)
    more.setdefault("in_specs", [vmem] * len(args))
    if "out_specs" not in more:
        more["out_specs"] = [vmem] * len(outs)
    return pl.pallas_call(
        kernel,
        out_shape=outs,
        compiler_params=pltpu.CompilerParams(vmem_limit_bytes=LIMIT),
        cost_estimate=pl.CostEstimate(flops=flops, bytes_accessed=1 << 20, transcendentals=0),
        name=name,
        **more,
    )(*args)


def body(field, saturation, solid_mask):
    count = lax.axis_size("tile")
    evens = [[t, t + 1] for t in range(0, count, 2)]
    odds = [pair for t in range(1, count - 1, 2) for pair in ((t, t + 1), (t + 1, t))]
    cells = STEPS * CHUNKS
    pack = STEPS + STEPS // 2
    args = [pltpu.with_memory_space_constraint(x, pltpu.HBM) for x in (field, saturation, solid_mask)]
    parts = [
        tiles(pack),
        tiles(STEPS, 3),
        tiles(2, STEPS),
        tiles(STEPS - 1, 8),
        tiles(STEPS, 3),
        tiles(3, 8),
        tiles(3),
        tiles(STEPS, 4),
        jax.ShapeDtypeStruct((8, LANES), jnp.float32),
    ]
    kept, turned, odd, *parts_early = call(
        early,
        [tiles(3, STEPS), tiles(pack), tiles(pack), *parts],
        args,
        "early",
        1 << 16,
        in_specs=[pl.BlockSpec(memory_space=pltpu.HBM)] * 3,
        scratch_shapes=[
            pltpu.VMEM((2, cells, LANES), jnp.float32),
            pltpu.VMEM((cells, LANES), jnp.float32),
            pltpu.VMEM((1, LANES), jnp.int32),
            pltpu.SemaphoreType.DMA((4,)),
        ],
    )
    odd = lax.ppermute(odd, "tile", odds)
    even, k_all, rhs, ab, dinv, ring, final, answer, share = call(
        late,
        parts,
        (kept, turned, *parts_early),
        "late",
        1 << 23,
        input_output_aliases={2 + j: j for j in range(len(parts))},
    )
    even = lax.all_gather(even, "tile", axis_index_groups=evens, axis=0)
    local_x, message = call(
        finish,
        [tiles(STEPS, 2), jax.ShapeDtypeStruct((8, LANES), jnp.float32)],
        (k_all, rhs, kept, ab, dinv, ring, final, share, odd, even),
        "finish",
        1 << 21,
    )
    both = lax.all_gather(message, "line", axis=0)
    return call(
        join,
        jax.ShapeDtypeStruct((2, cells, LANES), jnp.float32),
        (local_x, answer, both),
        "join",
        1 << 18,
        out_specs=pl.BlockSpec(memory_space=pltpu.HBM),
        scratch_shapes=[pltpu.VMEM((2, cells, LANES), jnp.float32), pltpu.SemaphoreType.DMA((2,))],
    )


def solution(mesh):
    in_specs = (P(None, "line", "tile"), P("line", "tile"), P("line", "tile"))
    out_specs = P(None, "line", "tile")
    return jax.shard_map(body, mesh=mesh, in_specs=in_specs, out_specs=out_specs, check_vma=False)
```

time: 18 us -> 17.3 us (0.961)
  starting transfers between devices: 7.28 us -> 6.77 us
  Pallas kernels: 2.76 us -> 2.54 us
    ppermute x1, starting transfers between devices: 7.28 us -> 6.77 us  [body(): odd = lax.ppermute(odd, 'tile', odds)]
    pallas_call x4, Pallas kernels: 2.76 us -> 2.54 us  [call(): pl.pallas_call(kernel, out_shape=outs, compiler_params=pltpu.CompilerPara...]
  transfers between devices with their start and end apart: 1 -> 1, of which waited for: 0 -> 0; matrix products, arithmetic and copies ran while one was open for 0% -> 0% of each run, Pallas kernels for 4% -> 0%
where the time goes in v2:
time: 17.3 us; the launch traced here: 17.1 us
  blocking collectives  7.74 us (45%)
  starting transfers between devices  6.77 us (39%)
  Pallas kernels  2.54 us (15%)
    ppermute x1, starting transfers between devices, body(): odd = lax.ppermute(odd, 'tile', odds)  6.77 us
    all_gather x1, blocking collectives, body(): even = lax.all_gather(even, 'tile', axis_index_groups=evens, axis=0)  4.21 us
    all_gather x1, blocking collectives, body(): both = lax.all_gather(message, 'line', axis=0)  3.54 us
    pallas_call x4, Pallas kernels, call(): pl.pallas_call(kernel, out_shape=outs, compiler_params=pltpu.CompilerPara...  2.54 us
  transfers between devices with their start and end apart: 1, of which 0 were waited for; matrix products, arithmetic and copies ran while one was open for 0% of the time, Pallas kernels for 0%

profile of v2, /device:TPU:449, one launch (start us, length us, event | category | flops | bytes accessed | tf_op | source)
XLA Modules:
  0.0 17.1 jit_solution(16531971014780450967)
XLA Ops:
  0.0 1.6 %early.1 = (f32[3,16,8,128]{3,2,1,0:T(8,128)S(1)}, f32[24,8,128]{2,1,0:T(8,128)S(1)}, f32[24,8,128]{2,1,0:T(8,128)S(1)}, f32[24,8,128]{2,1,0:T(8,128)S(1)}, f32[...) custom-call(f32[2,128,128]{2,1,0:T(8,128)} %field_hbm.1, ...), custom_call_target="tpu_custom_call" | custom-call | flops 65536 | bytes 1048576 | tf_op jit(solution)/shard_map/early/pallas_call | solution.py:382
  1.6 6.8 %collective-permute-start = (f32[24,8,128]{2,1,0:T(8,128)S(1)}, f32[24,8,128]{2,1,0:T(8,128)S(1)}, u32[]{:S(2)}, u32[]{:S(2)}) collective-permute-start(f32[24,8,128]{2,1,0:T(8,128)S(1)} %get-tuple-element.46), channel_id=1, source_target_pairs={{1,2},{2,1},{3,4},{4,3},{5,6},{6,5},{7,8},{8,7},{9,10},{10,9},{11,... | collective-permute-start | bytes 294920 | tf_op jit(solution)/shard_map/ppermute | solution.py:424
  8.4 4.2 %all-gather = f32[48,8,128]{2,1,0:T(8,128)S(1)} all-gather(f32[24,8,128]{2,1,0:T(8,128)S(1)} %get-tuple-element.47), channel_id=2, replica_groups={{0,1},{2,3},{4,5},{6,7},{8,9},{10,11},{12,13},{14,15},{16,17},{18,19},{..., dimensions={0}, use_global_device_ids=true | all-gather | bytes 294912 | tf_op jit(solution)/shard_map/all_gather | solution.py:433
  12.6 0.0 collective-permute-done.odd
  12.6 0.2 %finish.1 = (f32[16,2,8,128]{3,2,1,0:T(8,128)S(1)}, f32[8,128]{1,0:T(8,128)S(1)}) custom-call(f32[16,3,8,128]{3,2,1,0:T(8,128)S(1)} %get-tuple-element.39.k_all, f32[2,16,8,128]{3,2,1,0:T(8,128)S(1)} %get-tuple-element.40.rhs, f32[3,16,8,128]{3,2,1,0:T(8,128)S(1)} %get-tuple-element.28.kept, f32[15,8,8,128]{3,2,1,0:T(8,128)S(1)} %get-tuple-element.41.ab, ...), custom_call_target="tpu_custom_call" | custom-call | flops 2097152 | bytes 1048576 | tf_op jit(solution)/shard_map/finish/pallas_call | solution.py:382
  12.8 3.5 %all-gather.1 = f32[16,128]{1,0:T(8,128)S(1)} all-gather(f32[8,128]{1,0:T(8,128)S(1)} %get-tuple-element.50), channel_id=3, replica_groups=mesh['line'=2,'tile'=256] {'line'}, dimensions={0}, use_global_device_ids=true | all-gather | bytes 12288 | tf_op jit(solution)/shard_map/all_gather | solution.py:441
  16.4 0.7 %join.1 = f32[2,128,128]{2,1,0:T(8,128)} custom-call(f32[16,2,8,128]{3,2,1,0:T(8,128)S(1)} %get-tuple-element.48.local_x, f32[16,4,8,128]{3,2,1,0:T(8,128)S(1)} %get-tuple-element.49.answer, f32[2,8,128]{2,1,0:T(8,128)S(1)} %bitcast.3), custom_call_target="tpu_custom_call" | custom-call | flops 262144 | bytes 1048576 | tf_op jit(solution)/shard_map/join/pallas_call | solution.py:382
  (1 shorter events, 0.0 us)
Async XLA Ops:
  1.6 11.0 %collective-permute-start = (f32[24,8,128]{2,1,0:T(8,128)S(1)}, f32[24,8,128]{2,1,0:T(8,128)S(1)}, u32[]{:S(2)}, u32[]{:S(2)}) collective-permute-start(f32[24,8,128]{2,1,0:T(8,128)S(1)} %get-tuple-element.46), channel_id=1, source_target_pairs={{1,2},{2,1},{3,4},{4,3},{5,6},{6,5},{7,8},{8,7},{9,10},{10,9},{11,... | collective-permute-start | bytes 294920 | tf_op jit(solution)/shard_map/ppermute | solution.py:424

commit v3 on v2

v3 whole, which is shorter than its diff:
```python
import jax
import jax.numpy as jnp
from jax import lax
from jax.experimental import pallas as pl
from jax.experimental.pallas import tpu as pltpu
from jax.sharding import PartitionSpec as P

XS = 64
ZSTIFF = 2048
HALF = 0.5 * ZSTIFF
STEPS = 16
CHUNKS = 8
LANES = 128
TILE = (CHUNKS, LANES)
ROW = 4
SCALE = 0.4**0.5
CROSS = 0.1**0.5
GROW = HALF ** (1.0 / 3.0)
PACK = STEPS + STEPS // 2
LIMIT = 12 * 1024 * 1024


def mul(a, b):
    return (
        a[0] * b[0] + a[1] * b[2],
        a[0] * b[1] + a[1] * b[3],
        a[2] * b[0] + a[3] * b[2],
        a[2] * b[1] + a[3] * b[3],
    )


def wide(s):
    return (s[0], s[1], s[1], s[2])


def turn(a):
    return (a[0], a[2], a[1], a[3])


def apply(a, v):
    return (a[0] * v[0] + a[1] * v[1], a[2] * v[0] + a[3] * v[1])


def add(*items):
    total = items[0]
    for item in items[1:]:
        total = tuple(x + y for x, y in zip(total, item))
    return total


def symmetric(a, *more):
    return add(*((m[0], m[1], m[3]) for m in (a, *more)))


def inverse(s):
    scale = 1.0 / (s[0] * s[2] - s[1] * s[1])
    return (s[2] * scale, -s[1] * scale, s[0] * scale)


def conduct(signed, inside=None):
    dry = jnp.maximum(signed, 0.0)
    moist = HALF * 0.004 + dry * dry * dry
    pore = signed > 0.0
    heat = jnp.where(pore, HALF + (2.0 * HALF / GROW) * signed, 3.0 * HALF)
    cross = jnp.where(pore, CROSS * moist, 0.0)
    if inside is None:
        return (heat, cross, moist)
    return (jnp.where(inside, heat, 0.0), cross, jnp.where(inside, moist, 0.0))


def flux(k, drop):
    return (k[0] * drop[0] + k[1] * drop[1], k[1] * drop[0] + k[2] * drop[1])


def roll(x, shift, axis):
    return pltpu.roll(x, shift % x.shape[axis], axis)


def down(items, shift):
    return tuple(roll(x, shift, 0) for x in items)


def lanes():
    return lax.broadcasted_iota(jnp.int32, TILE, 1)


def chunks():
    return lax.broadcasted_iota(jnp.int32, TILE, 0)


def toward_odd():
    parity = lax.rem(lax.axis_index("tile"), 2)
    return (lanes() >= XS) == (parity == 1)


def load(ref, *index):
    return tuple(ref[(*index, j)] for j in range(ref.shape[len(index)]))


def store(ref, index, items):
    for j, item in enumerate(items):
        ref[(*index, j)] = item


def levels():
    stride = 1
    while stride < STEPS:
        yield stride, range(0, STEPS, 2 * stride), range(stride, STEPS, 2 * stride)
        stride *= 2


def rows_of():
    place, at = {}, 0
    for stride, kept, _ in levels():
        for step in kept:
            place[stride, step] = at
            at += 1
    return place


PLACE = rows_of()


def pack_even(kept, turned, even):
    near = toward_odd()
    half = STEPS // 2
    for i in range(STEPS):
        even[i] = jnp.where(near, turned[i], kept[0, i])
    for i in range(half):
        even[STEPS + i] = jnp.where(near, turned[STEPS + i], kept[2, i])


def signs(mask, sign):
    sign[...] = jnp.where(jnp.broadcast_to(mask[...], TILE) > 0, -GROW, GROW)


def prepare(field, sat, sign, kept, turned, odd):
    near = toward_odd()
    half = STEPS // 2
    rows = [pl.ds(i, CHUNKS, stride=STEPS) for i in range(STEPS)]
    sign = sign[...]
    for i in range(STEPS):
        f1 = field[1, rows[i], :] * (1.0 / SCALE)
        kept[1, i] = f1
        turned[i] = roll(f1, XS, 1)
    for i in range(STEPS):
        s = sat[rows[i], :] * sign
        kept[2, i] = s
        if i >= half:
            high = roll(s, XS, 1)
            turned[STEPS + i - half] = high
            odd[STEPS + i - half] = jnp.where(near, kept[2, i - half], high)
    for i in range(STEPS):
        f0 = field[0, rows[i], :]
        kept[0, i] = f0
        odd[i] = jnp.where(near, f0, turned[i])


def tile():
    return lax.axis_index("tile")


def at_row_end():
    place = lax.rem(lax.axis_index("tile"), ROW)
    return jnp.logical_or(place == 0, place == ROW - 1)


def inner(field_hbm, sat_hbm, mask_hbm, kept, turned, odd, even, fbuf, sbuf, mbuf, gbuf, sems):
    @pl.when(jnp.logical_not(at_row_end()))
    def _():
        copies = [
            pltpu.make_async_copy(field_hbm, fbuf, sems.at[0]),
            pltpu.make_async_copy(sat_hbm, sbuf, sems.at[1]),
            pltpu.make_async_copy(mask_hbm, mbuf, sems.at[2]),
        ]
        for copy in copies:
            copy.start()
        for copy in copies:
            copy.wait()
        signs(mbuf, gbuf)
        prepare(fbuf, sbuf, gbuf, kept, turned, odd)
        pack_even(kept, turned, even)

    @pl.when(jnp.logical_and(tile() >= 1, tile() <= 2))
    def _():
        for i in range(PACK):
            odd[i], even[i] = even[i], odd[i]


def ends(field, sat, sign, kept_in, turned_in, odd_in, kept, turned, odd):
    @pl.when(at_row_end())
    def _():
        prepare(field, sat, sign, kept, turned, odd)

    @pl.when(tile() == 0)
    def _():
        pack_even(kept, turned, odd)


def third(kept, turned, first, arrived, out):
    @pl.when(tile() != 1)
    def _():
        pack_even(kept, turned, out)

    @pl.when(tile() == 1)
    def _():
        for i in range(PACK):
            out[i] = first[i]


def local(kept, turned, k_all, rhs, ab, dinv, ring, final, answer, share):
    line = lax.axis_index("line")
    first, last = chunks() == 0, chunks() == CHUNKS - 1
    low_line, high_line = line == 0, line == 1
    column = lax.rem(lanes(), XS)
    west_end, east_end = column == 0, column == XS - 1
    half = STEPS // 2

    k = []
    for i in range(STEPS):
        s = kept[2, i]
        ki = conduct(s)
        k.append(ki)
        store(k_all, (i,), ki)
        f = (kept[0, i], kept[1, i])
        far = (roll(f[0], XS, 1), turned[i])
        far_s = turned[STEPS + i - half] if i >= half else roll(s, XS, 1)
        total = flux(add(ki, conduct(far_s)), (far[0] - f[0], far[1] - f[1]))
        west_k = conduct(roll(s, 1, 1))
        west = flux(add(ki, west_k), (roll(f[0], 1, 1) - f[0], roll(f[1], 1, 1) - f[1]))
        edge = flux(ki, f)
        west = tuple(jnp.where(west_end, -e, w) for e, w in zip(edge, west))
        east = tuple(jnp.where(east_end, e, roll(w, -1, 1)) for e, w in zip(edge, west))
        for j in range(2):
            rhs[j, i] = f[j] + (total[j] + (west[j] - east[j]))

    upper = {i: wide(add(k[i], k[i + 1])) for i in range(STEPS - 1)}
    upper[STEPS - 1] = wide(tuple(jnp.where(last, 0.0, x) for x in add(k[-1], down(k[0], -1))))
    bottom = jnp.logical_and(first, low_line)
    top = jnp.logical_and(last, high_line)
    bottom = tuple(jnp.where(bottom, x, 0.0) for x in k[0])
    top = tuple(jnp.where(top, x, 0.0) for x in k[-1])
    excess = {}

    for stride, keep, drop in levels():
        lower = {}
        for i in (*keep, *drop):
            left = i - stride
            lower[i] = turn(upper[left] if left >= 0 else down(upper[left + STEPS], 1))
        inv = {}
        for i in drop:
            if stride == 1:
                d = symmetric(lower[i], upper[i])
                d = (d[0] + 1.0, d[1], d[2] + 1.0)
                if i == STEPS - 1:
                    d = add(d, top)
            else:
                d = symmetric(excess[i], lower[i], upper[i])
            inv[i] = inverse(d)
            store(dinv, (i,), inv[i])
        for i in keep:
            right, left = i + stride, i - stride
            if left < 0:
                before = wide(down(inv[left + STEPS], 1))
            else:
                before = wide(inv[left])
            a = mul(lower[i], before)
            b = mul(upper[i], wide(inv[right]))
            store(ab, (PLACE[stride, i],), (*a, *b))
            if stride == 1:
                more = add(a, b)
                more = (more[0] + 1.0, more[1], more[2], more[3] + 1.0)
                if i == 0:
                    more = add(more, wide(bottom))
                if right == STEPS - 1:
                    more = add(more, mul(b, wide(top)))
            else:
                prev = excess[left] if left >= 0 else down(excess[left + STEPS], 1)
                more = add(excess[i], mul(a, prev), mul(b, excess[right]))
            excess[i] = more
            upper[i] = mul(b, upper[right])

    start = jnp.where(jnp.logical_and(high_line, first), 1.0, 0.0)
    end = jnp.logical_and(low_line, last)
    one = jnp.where(end, 1.0, 0.0)
    none = jnp.zeros(TILE, jnp.float32)
    source = (one, none, none, one)
    sides = {STEPS - 1: source}
    for stride, keep, _ in levels():
        b = load(ab, PLACE[stride, keep[-1]])[4:8]
        source = tuple(jnp.where(end, x, 0.0) for x in b) if stride == 1 else mul(b, source)
        sides[keep[-1]] = source
    vec = (source[0] + start, source[1], source[2], source[3] + start)

    up, ex = upper[0], excess[0]
    low = turn(down(up, 1))
    shift, place = 1, 0
    while shift < CHUNKS:
        inv = inverse(symmetric(ex, low, up))
        a = mul(low, wide(down(inv, shift)))
        b = mul(up, wide(down(inv, -shift)))
        store(ring, (place,), (*a, *b))
        vec = add(vec, mul(a, down(vec, shift)), mul(b, down(vec, -shift)))
        ex = add(ex, mul(a, down(ex, shift)), mul(b, down(ex, -shift)))
        up = mul(b, down(up, -shift))
        shift *= 2
        place += 1
        low = turn(down(up, shift))
    inv = inverse((ex[0], ex[1], ex[3]))
    store(final, (), inv)
    w = {0: mul(wide(inv), vec)}
    for stride, keep, drop in reversed(list(levels())):
        for i in drop:
            left, right = i - stride, i + stride
            prev = turn(load(ab, PLACE[stride, left])[4:8])
            if right < STEPS:
                after, later = turn(load(ab, PLACE[stride, right])[0:4]), w[right]
            else:
                after, later = turn(down(load(ab, PLACE[stride, 0])[0:4], -1)), down(w[0], -1)
            w[i] = add(mul(prev, w[left]), mul(after, later))
            if i in sides:
                w[i] = add(w[i], mul(wide(load(dinv, i)), sides[i]))
    for i in range(STEPS):
        for j, x in enumerate((w[i][0], w[i][1], SCALE * w[i][2], SCALE * w[i][3])):
            answer[j, pl.ds(i, CHUNKS, stride=STEPS), :] = x

    tail = down((w[STEPS - 1][0], w[STEPS - 1][1], w[STEPS - 1][3], kept[2, STEPS - 1]), 1)
    head = (w[0][0], w[0][1], w[0][3], kept[2, 0])
    for j, (x, y) in enumerate(zip(head, tail)):
        share[pl.ds(2 + j, 1), :] = jnp.where(low_line, y, x)[0:1]
    share[pl.ds(0, 2), :] = none[0:2]
    share[pl.ds(6, 2), :] = none[0:2]


def finish(k_all, rhs, kept, ab, dinv, ring, final, share, one, two, four, three, local_x, message):
    rest = (k_all, rhs, kept, ab, dinv, ring, final, share, local_x, message)

    @pl.when(tile() >= ROW)
    def _():
        end = at_row_end()
        solve(lambda i: (two[i], jnp.where(end, one[i], three[i])), *rest)

    @pl.when(tile() < ROW)
    def _():
        at = tile()

        def halo(i):
            odd = jnp.where(at <= 1, one[i], jnp.where(at == 2, three[i], two[i]))
            return odd, jnp.where(at <= 1, two[i], four[i])

        solve(halo, *rest)


def solve(halo, k_all, rhs, kept, ab, dinv, ring, final, share, local_x, message):
    line = lax.axis_index("line")
    near = toward_odd()
    alone = jnp.logical_or(tile() == 0, tile() == lax.axis_size("tile") - 1)
    inside = jnp.logical_not(jnp.logical_and(near, alone))
    half = STEPS // 2
    far_s, far_0, far_1 = [None] * STEPS, [], []
    for i in range(half):
        o, e = halo(STEPS + i)
        far_s[i] = roll(jnp.where(near, e, o), XS, 1)
        far_s[i + half] = jnp.where(near, o, e)
    for i in range(STEPS):
        o, e = halo(i)
        far_0.append(roll(jnp.where(near, e, o), XS, 1))
        far_1.append(jnp.where(near, o, e))
    b = {}
    for i in range(STEPS):
        drop = (far_0[i] - kept[0, i], far_1[i] - kept[1, i])
        total = flux(add(load(k_all, i), conduct(far_s[i], inside)), drop)
        b[i] = (rhs[0, i] + total[0], rhs[1, i] + total[1])
    for stride, keep, drop in levels():
        for i in keep:
            left = i - stride
            prev = b[left] if left >= 0 else down(b[left + STEPS], 1)
            c = load(ab, PLACE[stride, i])
            b[i] = add(b[i], apply(c[0:4], prev), apply(c[4:8], b[i + stride]))
    vec = b[0]
    shift, place = 1, 0
    while shift < CHUNKS:
        c = load(ring, place)
        vec = add(vec, apply(c[0:4], down(vec, shift)), apply(c[4:8], down(vec, -shift)))
        shift *= 2
        place += 1
    x = {0: apply(wide(load(final)), vec)}
    for stride, keep, drop in reversed(list(levels())):
        for i in drop:
            left, right = i - stride, i + stride
            prev = turn(load(ab, PLACE[stride, left])[4:8])
            if right < STEPS:
                after, later = turn(load(ab, PLACE[stride, right])[0:4]), x[right]
            else:
                after, later = turn(down(load(ab, PLACE[stride, 0])[0:4], -1)), down(x[0], -1)
            x[i] = add(apply(wide(load(dinv, i)), b[i]), apply(prev, x[left]), apply(after, later))
    message[...] = share[...]
    tail = down(x[STEPS - 1], 1)
    for j in range(2):
        message[pl.ds(j, 1), :] = jnp.where(line == 0, tail[j], x[0][j])[0:1]
    for i in range(STEPS):
        here = pl.ds(i, CHUNKS, stride=STEPS)
        local_x[0, here, :] = x[i][0]
        local_x[1, here, :] = SCALE * x[i][1]


def join(local_x, answer, both, out_hbm, out, sems):
    line = lax.axis_index("line")

    def row(who, j):
        return jnp.broadcast_to(both[who, pl.ds(j, 1), :], TILE)

    sign = jnp.where(line == 0, 1.0, -1.0)
    drop = tuple(sign * (row(1, j) - row(0, j)) for j in range(2))
    reach = wide(tuple(row(0, 2 + j) + row(1, 2 + j) for j in range(3)))
    face = add(conduct(row(0, 5)), conduct(row(1, 5)))
    m = mul(wide(face), reach)
    m = (m[0] + 1.0, m[1], m[2], m[3] + 1.0)
    push = flux(face, drop)
    scale = 1.0 / (m[0] * m[3] - m[1] * m[2])
    through = ((m[3] * push[0] - m[1] * push[1]) * scale, (m[0] * push[1] - m[2] * push[0]) * scale)

    copies = [pltpu.make_async_copy(out.at[j], out_hbm.at[j], sems.at[j]) for j in range(2)]
    for j in range(2):
        for i in range(STEPS):
            here = pl.ds(i * CHUNKS, CHUNKS)
            change = answer[2 * j, here, :] * through[0] + answer[2 * j + 1, here, :] * through[1]
            out[j, here, :] = local_x[j, here, :] + change
        copies[j].start()
    for copy in copies:
        copy.wait()


def tiles(*lead):
    return jax.ShapeDtypeStruct((*lead, *TILE), jnp.float32)


def call(kernel, outs, args, name, flops, **more):
    vmem = pl.BlockSpec(memory_space=pltpu.VMEM)
    more.setdefault("in_specs", [vmem] * len(args))
    if "out_specs" not in more:
        more["out_specs"] = [vmem] * len(outs)
    return pl.pallas_call(
        kernel,
        out_shape=outs,
        compiler_params=pltpu.CompilerParams(vmem_limit_bytes=LIMIT),
        cost_estimate=pl.CostEstimate(flops=flops, bytes_accessed=1 << 20, transcendentals=0),
        name=name,
        **more,
    )(*args)


def moves(count):
    first, second, third = [(2, 1)], [(0, 1), (1, 0)], [(1, 2)]
    for t in range(ROW, count, ROW):
        first += [(t + 1, t), (t + 2, t + 3)]
        second += [(t - 1, t), (t, t - 1), (t + 1, t + 2), (t + 2, t + 1)]
        third += [(t, t + 1), (t + 3, t + 2)]
    return first, second, third, [(2, 3), (3, 2)]


def body(field, saturation, solid_mask):
    first, second, third_moves, fourth_moves = moves(lax.axis_size("tile"))
    cells = STEPS * CHUNKS
    in_hbm = [pltpu.with_memory_space_constraint(x, pltpu.HBM) for x in (field, saturation, solid_mask)]
    kept, turned, two, one = call(
        inner,
        [tiles(3, STEPS), tiles(PACK), tiles(PACK), tiles(PACK)],
        in_hbm,
        "inner",
        1 << 16,
        in_specs=[pl.BlockSpec(memory_space=pltpu.HBM)] * 3,
        scratch_shapes=[
            pltpu.VMEM((2, cells, LANES), jnp.float32),
            pltpu.VMEM((cells, LANES), jnp.float32),
            pltpu.VMEM((1, LANES), jnp.int32),
            pltpu.VMEM(TILE, jnp.float32),
            pltpu.SemaphoreType.DMA((3,)),
        ],
    )
    from_one = lax.ppermute(one, "tile", first)
    (sign,) = call(signs, [tiles()], (solid_mask,), "signs", 1 << 8)
    kept, turned, two = call(
        ends,
        [tiles(3, STEPS), tiles(PACK), tiles(PACK)],
        (field, saturation, sign, kept, turned, two),
        "ends",
        1 << 16,
        input_output_aliases={3: 0, 4: 1, 5: 2},
    )
    from_two = lax.ppermute(two, "tile", second)
    (three,) = call(third, [tiles(PACK)], (kept, turned, one, from_one), "third", 1 << 12)
    from_three = lax.ppermute(three, "tile", third_moves)
    from_four = lax.ppermute(three, "tile", fourth_moves)
    k_all, rhs, ab, dinv, ring, final, answer, share = call(
        local,
        [
            tiles(STEPS, 3),
            tiles(2, STEPS),
            tiles(STEPS - 1, 8),
            tiles(STEPS, 3),
            tiles(3, 8),
            tiles(3),
            jax.ShapeDtypeStruct((4, cells, LANES), jnp.float32),
            jax.ShapeDtypeStruct((8, LANES), jnp.float32),
        ],
        (kept, turned),
        "local",
        1 << 23,
    )
    local_x, message = call(
        finish,
        [jax.ShapeDtypeStruct((2, cells, LANES), jnp.float32), jax.ShapeDtypeStruct((8, LANES), jnp.float32)],
        (k_all, rhs, kept, ab, dinv, ring, final, share, from_one, from_two, from_four, from_three),
        "finish",
        1 << 21,
    )
    both = lax.all_gather(message, "line", axis=0)
    return call(
        join,
        jax.ShapeDtypeStruct((2, cells, LANES), jnp.float32),
        (local_x, answer, both),
        "join",
        1 << 18,
        out_specs=pl.BlockSpec(memory_space=pltpu.HBM),
        scratch_shapes=[pltpu.VMEM((2, cells, LANES), jnp.float32), pltpu.SemaphoreType.DMA((2,))],
    )


def solution(mesh):
    in_specs = (P(None, "line", "tile"), P("line", "tile"), P("line", "tile"))
    out_specs = P(None, "line", "tile")
    return jax.shard_map(body, mesh=mesh, in_specs=in_specs, out_specs=out_specs, check_vma=False)
```

time: 17.3 us -> 17.1 us (0.988)
  the two profiles are of different devices: /device:TPU:449 before, /device:TPU:1 now
where the time goes in v3:
time: 17.1 us; the launch traced here: 16.9 us
  starting transfers between devices  7.53 us (44%)
  blocking collectives  7.47 us (44%)
  Pallas kernels  1.71 us (10%)
    all_gather x1, blocking collectives, body(): both = lax.all_gather(message, 'line', axis=0)  7.47 us
    ppermute x1, starting transfers between devices, body(): from_two = lax.ppermute(two, 'tile', second)  5.4 us
    pallas_call x7, Pallas kernels, call(): pl.pallas_call(kernel, out_shape=outs, compiler_params=pltpu.CompilerPara...  1.71 us
    ppermute x1, starting transfers between devices, body(): from_one = lax.ppermute(one, 'tile', first)  0.8 us
    ppermute x1, starting transfers between devices, body(): from_three = lax.ppermute(three, 'tile', third_moves)  0.67 us
    ppermute x1, starting transfers between devices, body(): from_four = lax.ppermute(three, 'tile', fourth_moves)  0.67 us
  transfers between devices with their start and end apart: 4, of which 0 were waited for; matrix products, arithmetic and copies ran while one was open for 0% of the time, Pallas kernels for 4%

profile of v3, /device:TPU:1, one launch (start us, length us, event | category | flops | bytes accessed | tf_op | source)
XLA Modules:
  0.0 16.9 jit_solution(4536152292525048189)
XLA Ops:
  0.0 0.0 copy-start.1
  0.0 0.0 copy-start
  0.0 0.0 copy-start.2
  0.1 0.8 %collective-permute-start = (f32[24,8,128]{2,1,0:T(8,128)S(1)}, f32[24,8,128]{2,1,0:T(8,128)S(1)}, u32[]{:S(2)}, u32[]{:S(2)}) collective-permute-start(f32[24,8,128]{2,1,0:T(8,128)S(1)} %get-tuple-element.34.first), channel_id=1, source_target_pairs={{2,1},{5,4},{6,7},{9,8},{10,11},{13,12},{14,15},{17,16},{18,19},{2... | collective-permute-start | bytes 294920 | tf_op jit(solution)/shard_map/ppermute | solution.py:481
  0.9 0.0 copy-done.2
  0.9 0.0 copy-done.1
  0.9 0.1 copy-done
  0.9 0.1 ends.1
  1.1 5.4 %collective-permute-start.1 = (f32[24,8,128]{2,1,0:T(8,128)S(1)}, f32[24,8,128]{2,1,0:T(8,128)S(1)}, u32[]{:S(2)}, u32[]{:S(2)}) collective-permute-start(f32[24,8,128]{2,1,0:T(8,128)S(1)} %get-tuple-element.35), channel_id=1, source_target_pairs={{0,1},{1,0},{3,4},{4,3},{5,6},{6,5},{7,8},{8,7},{9,10},{10,9},{11,... | collective-permute-start | bytes 294920 | tf_op jit(solution)/shard_map/ppermute | solution.py:491
  6.5 0.0 collective-permute-done.arrived.one
  6.5 0.7 %collective-permute-start.3 = (f32[24,8,128]{2,1,0:T(8,128)S(1)}, f32[24,8,128]{2,1,0:T(8,128)S(1)}, u32[]{:S(2)}, u32[]{:S(2)}) collective-permute-start(f32[24,8,128]{2,1,0:T(8,128)S(1)} %third.1), channel_id=1, source_target_pairs={{1,2},{4,5},{7,6},{8,9},{11,10},{12,13},{15,14},{16,17},{19,18},{2... | collective-permute-start | bytes 294920 | tf_op jit(solution)/shard_map/ppermute | solution.py:493
  7.2 0.7 %collective-permute-start.2 = (f32[24,8,128]{2,1,0:T(8,128)S(1)}, f32[24,8,128]{2,1,0:T(8,128)S(1)}, u32[]{:S(2)}, u32[]{:S(2)}) collective-permute-start(f32[24,8,128]{2,1,0:T(8,128)S(1)} %third.1), channel_id=1, source_target_pairs={{2,3},{3,2},{258,259},{259,258}} | collective-permute-start | bytes 294920 | tf_op jit(solution)/shard_map/ppermute | solution.py:494
  7.9 0.6 %local.1 = (f32[16,3,8,128]{3,2,1,0:T(8,128)S(1)}, f32[2,16,8,128]{3,2,1,0:T(8,128)S(1)}, f32[15,8,8,128]{3,2,1,0:T(8,128)S(1)}, f32[16,3,8,128]{3,2,1,0:T(8,128...) custom-call(f32[3,16,8,128]{3,2,1,0:T(8,128)S(1)} %get-tuple-element, ...), custom_call_target="tpu_custom_call" | custom-call | flops 8388608 | bytes 1048576 | tf_op jit(solution)/shard_map/local/pallas_call | solution.py:443
  8.4 0.0 collective-permute-done.1.two
  8.5 0.0 collective-permute-done.3.three
  8.5 0.0 collective-permute-done.2.four
  8.5 0.3 %finish.1 = (f32[2,128,128]{2,1,0:T(8,128)S(1)}, f32[8,128]{1,0:T(8,128)S(1)}) custom-call(f32[16,3,8,128]{3,2,1,0:T(8,128)S(1)} %get-tuple-element.27.k_all, f32[2,16,8,128]{3,2,1,0:T(8,128)S(1)} %get-tuple-element.28.rhs, f32[3,16,8,128]{3,2,1,0:T(8,128)S(1)} %get-tuple-element.25.kept, f32[15,8,8,128]{3,2,1,0:T(8,128)S(1)} %get-tuple-element.29.ab, ...), custom_call_target="tpu_custom_call" | custom-call | flops 2097152 | bytes 1048576 | tf_op jit(solution)/shard_map/finish/pallas_call | solution.py:443
  8.7 7.5 %all-gather = f32[16,128]{1,0:T(8,128)S(1)} all-gather(f32[8,128]{1,0:T(8,128)S(1)} %get-tuple-element.38), channel_id=2, replica_groups=mesh['line'=2,'tile'=256] {'line'}, dimensions={0}, use_global_device_ids=true | all-gather | bytes 12288 | tf_op jit(solution)/shard_map/all_gather | solution.py:518
  16.2 0.7 %join.1 = f32[2,128,128]{2,1,0:T(8,128)} custom-call(f32[2,128,128]{2,1,0:T(8,128)S(1)} %get-tuple-element.36.local_x, f32[4,128,128]{2,1,0:T(8,128)S(1)} %get-tuple-element.37.answer, f32[2,8,128]{2,1,0:T(8,128)S(1)} %bitcast.1), custom_call_target="tpu_custom_call" | custom-call | flops 262144 | bytes 1048576 | tf_op jit(solution)/shard_map/join/pallas_call | solution.py:443
  (3 shorter events, 0.1 us)
Async XLA Ops:
  0.0 0.9 %copy-start.1 = (f32[128,128]{1,0:T(8,128)S(1)}, f32[128,128]{1,0:T(8,128)}, u32[]{:S(2)}) copy-start(f32[128,128]{1,0:T(8,128)} %sat.1) | copy-start | bytes 196612
  0.0 0.9 %copy-start = (f32[2,128,128]{2,1,0:T(8,128)S(1)}, f32[2,128,128]{2,1,0:T(8,128)}, u32[]{:S(2)}) copy-start(f32[2,128,128]{2,1,0:T(8,128)} %field.1) | copy-start | bytes 393220
  0.0 0.8 %copy-start.2 = (s32[1,128]{1,0:T(1,128)S(1)}, s32[1,128]{1,0:T(1,128)}, u32[]{:S(2)}) copy-start(s32[1,128]{1,0:T(1,128)} %mask_hbm.1) | copy-start | bytes 1540
  0.1 6.4 %collective-permute-start = (f32[24,8,128]{2,1,0:T(8,128)S(1)}, f32[24,8,128]{2,1,0:T(8,128)S(1)}, u32[]{:S(2)}, u32[]{:S(2)}) collective-permute-start(f32[24,8,128]{2,1,0:T(8,128)S(1)} %get-tuple-element.34.first), channel_id=1, source_target_pairs={{2,1},{5,4},{6,7},{9,8},{10,11},{13,12},{14,15},{17,16},{18,19},{2... | collective-permute-start | bytes 294920 | tf_op jit(solution)/shard_map/ppermute | solution.py:481
  1.1 7.4 %collective-permute-start.1 = (f32[24,8,128]{2,1,0:T(8,128)S(1)}, f32[24,8,128]{2,1,0:T(8,128)S(1)}, u32[]{:S(2)}, u32[]{:S(2)}) collective-permute-start(f32[24,8,128]{2,1,0:T(8,128)S(1)} %get-tuple-element.35), channel_id=1, source_target_pairs={{0,1},{1,0},{3,4},{4,3},{5,6},{6,5},{7,8},{8,7},{9,10},{10,9},{11,... | collective-permute-start | bytes 294920 | tf_op jit(solution)/shard_map/ppermute | solution.py:491
  6.5 1.9 %collective-permute-start.3 = (f32[24,8,128]{2,1,0:T(8,128)S(1)}, f32[24,8,128]{2,1,0:T(8,128)S(1)}, u32[]{:S(2)}, u32[]{:S(2)}) collective-permute-start(f32[24,8,128]{2,1,0:T(8,128)S(1)} %third.1), channel_id=1, source_target_pairs={{1,2},{4,5},{7,6},{8,9},{11,10},{12,13},{15,14},{16,17},{19,18},{2... | collective-permute-start | bytes 294920 | tf_op jit(solution)/shard_map/ppermute | solution.py:493
  7.2 1.3 %collective-permute-start.2 = (f32[24,8,128]{2,1,0:T(8,128)S(1)}, f32[24,8,128]{2,1,0:T(8,128)S(1)}, u32[]{:S(2)}, u32[]{:S(2)}) collective-permute-start(f32[24,8,128]{2,1,0:T(8,128)S(1)} %third.1), channel_id=1, source_target_pairs={{2,3},{3,2},{258,259},{259,258}} | collective-permute-start | bytes 294920 | tf_op jit(solution)/shard_map/ppermute | solution.py:494

commit v4 on v3

--- a/solution.py
+++ b/solution.py
@@ -160,6 +160,10 @@
     return lax.axis_index("tile")
 
 
+def line():
+    return lax.axis_index("line")
+
+
 def at_row_end():
     place = lax.rem(lax.axis_index("tile"), ROW)
     return jnp.logical_or(place == 0, place == ROW - 1)
@@ -181,7 +185,7 @@
         prepare(fbuf, sbuf, gbuf, kept, turned, odd)
         pack_even(kept, turned, even)
 
-    @pl.when(jnp.logical_and(tile() >= 1, tile() <= 2))
+    @pl.when(jnp.logical_or(tile() == 2, jnp.logical_and(tile() == 1, line() == 1)))
     def _():
         for i in range(PACK):
             odd[i], even[i] = even[i], odd[i]
@@ -197,21 +201,22 @@
         pack_even(kept, turned, odd)
 
 
-def third(kept, turned, first, arrived, out):
-    @pl.when(tile() != 1)
+def third(kept, turned, arrived, out):
+    relay = jnp.logical_and(tile() == 0, line() == 1)
+
+    @pl.when(jnp.logical_not(relay))
     def _():
         pack_even(kept, turned, out)
 
-    @pl.when(tile() == 1)
+    @pl.when(relay)
     def _():
         for i in range(PACK):
-            out[i] = first[i]
+            out[i] = arrived[i]
 
 
 def local(kept, turned, k_all, rhs, ab, dinv, ring, final, answer, share):
-    line = lax.axis_index("line")
     first, last = chunks() == 0, chunks() == CHUNKS - 1
-    low_line, high_line = line == 0, line == 1
+    low_line, high_line = line() == 0, line() == 1
     column = lax.rem(lanes(), XS)
     west_end, east_end = column == 0, column == XS - 1
     half = STEPS // 2
@@ -332,27 +337,29 @@
     share[pl.ds(6, 2), :] = none[0:2]
 
 
-def finish(k_all, rhs, kept, ab, dinv, ring, final, share, one, two, four, three, local_x, message):
+def finish(k_all, rhs, kept, ab, dinv, ring, final, share, one, two, three, local_x, message):
     rest = (k_all, rhs, kept, ab, dinv, ring, final, share, local_x, message)
 
     @pl.when(tile() >= ROW)
     def _():
-        end = at_row_end()
-        solve(lambda i: (two[i], jnp.where(end, one[i], three[i])), *rest)
+        place = lax.rem(tile(), ROW)
+        solve(lambda i: (two[i], jnp.where(place == 0, one[i], three[i])), *rest)
 
     @pl.when(tile() < ROW)
     def _():
-        at = tile()
+        at, high = tile(), line() == 1
 
         def halo(i):
-            odd = jnp.where(at <= 1, one[i], jnp.where(at == 2, three[i], two[i]))
-            return odd, jnp.where(at <= 1, two[i], four[i])
+            odd = jnp.where(at == 1, one[i], two[i])
+            odd = jnp.where(jnp.logical_and(high, at == 2), one[i], odd)
+            odd = jnp.where(jnp.logical_and(high, at == 0), three[i], odd)
+            even = jnp.where(jnp.logical_or(at == 1, jnp.logical_and(high, at == 0)), two[i], three[i])
+            return odd, even
 
         solve(halo, *rest)
 
 
 def solve(halo, k_all, rhs, kept, ab, dinv, ring, final, share, local_x, message):
-    line = lax.axis_index("line")
     near = toward_odd()
     alone = jnp.logical_or(tile() == 0, tile() == lax.axis_size("tile") - 1)
     inside = jnp.logical_not(jnp.logical_and(near, alone))
@@ -397,7 +404,7 @@
     message[...] = share[...]
     tail = down(x[STEPS - 1], 1)
     for j in range(2):
-        message[pl.ds(j, 1), :] = jnp.where(line == 0, tail[j], x[0][j])[0:1]
+        message[pl.ds(j, 1), :] = jnp.where(line() == 0, tail[j], x[0][j])[0:1]
     for i in range(STEPS):
         here = pl.ds(i, CHUNKS, stride=STEPS)
         local_x[0, here, :] = x[i][0]
@@ -405,12 +412,10 @@
 
 
 def join(local_x, answer, both, out_hbm, out, sems):
-    line = lax.axis_index("line")
-
     def row(who, j):
         return jnp.broadcast_to(both[who, pl.ds(j, 1), :], TILE)
 
-    sign = jnp.where(line == 0, 1.0, -1.0)
+    sign = jnp.where(line() == 0, 1.0, -1.0)
     drop = tuple(sign * (row(1, j) - row(0, j)) for j in range(2))
     reach = wide(tuple(row(0, 2 + j) + row(1, 2 + j) for j in range(3)))
     face = add(conduct(row(0, 5)), conduct(row(1, 5)))
@@ -451,16 +456,23 @@
 
 
 def moves(count):
-    first, second, third = [(2, 1)], [(0, 1), (1, 0)], [(1, 2)]
-    for t in range(ROW, count, ROW):
-        first += [(t + 1, t), (t + 2, t + 3)]
-        second += [(t - 1, t), (t, t - 1), (t + 1, t + 2), (t + 2, t + 1)]
-        third += [(t, t + 1), (t + 3, t + 2)]
-    return first, second, third, [(2, 3), (3, 2)]
+    ops = [[], [], []]
+    for base in (0, count):
+        for t in range(base, base + count, ROW):
+            ops[2] += [(t + 2, t + 3), (t + 3, t + 2)]
+            if t > base:
+                ops[0].append((t + 1, t))
+                ops[1] += [(t - 1, t), (t, t - 1), (t + 1, t + 2), (t + 2, t + 1)]
+                ops[2].append((t, t + 1))
+    ops[0] += [(1, count), (2, 1), (count + 1, count + 2), (count + 2, count + 1)]
+    ops[1] += [(0, 1), (1, 2), (count, count + 1), (count + 1, count)]
+    ops[2].append((count, 0))
+    return ops
 
 
 def body(field, saturation, solid_mask):
-    first, second, third_moves, fourth_moves = moves(lax.axis_size("tile"))
+    ops = moves(lax.axis_size("tile"))
+    both_axes = ("line", "tile")
     cells = STEPS * CHUNKS
     in_hbm = [pltpu.with_memory_space_constraint(x, pltpu.HBM) for x in (field, saturation, solid_mask)]
     kept, turned, two, one = call(
@@ -478,7 +490,7 @@
             pltpu.SemaphoreType.DMA((3,)),
         ],
     )
-    from_one = lax.ppermute(one, "tile", first)
+    from_one = lax.ppermute(one, both_axes, ops[0])
     (sign,) = call(signs, [tiles()], (solid_mask,), "signs", 1 << 8)
     kept, turned, two = call(
         ends,
@@ -488,10 +500,9 @@
         1 << 16,
         input_output_aliases={3: 0, 4: 1, 5: 2},
     )
-    from_two = lax.ppermute(two, "tile", second)
-    (three,) = call(third, [tiles(PACK)], (kept, turned, one, from_one), "third", 1 << 12)
-    from_three = lax.ppermute(three, "tile", third_moves)
-    from_four = lax.ppermute(three, "tile", fourth_moves)
+    from_two = lax.ppermute(two, both_axes, ops[1])
+    (three,) = call(third, [tiles(PACK)], (kept, turned, from_one), "third", 1 << 12)
+    from_three = lax.ppermute(three, both_axes, ops[2])
     k_all, rhs, ab, dinv, ring, final, answer, share = call(
         local,
         [
@@ -511,7 +522,7 @@
     local_x, message = call(
         finish,
         [jax.ShapeDtypeStruct((2, cells, LANES), jnp.float32), jax.ShapeDtypeStruct((8, LANES), jnp.float32)],
-        (k_all, rhs, kept, ab, dinv, ring, final, share, from_one, from_two, from_four, from_three),
+        (k_all, rhs, kept, ab, dinv, ring, final, share, from_one, from_two, from_three),
         "finish",
         1 << 21,
     )

time: 17.1 us -> 16.9 us (0.988)
  the two profiles are of different devices: /device:TPU:1 before, /device:TPU:257 now
where the time goes in v4:
time: 16.9 us; the launch traced here: 16.7 us
  starting transfers between devices  8.51 us (50%)
  blocking collectives  3.32 us (20%)
  waiting for transfers between devices  3.08 us (18%)
  Pallas kernels  1.71 us (10%)
    ppermute x1, starting transfers between devices, body(): from_two = lax.ppermute(two, both_axes, ops[1])  5.79 us
    all_gather x1, blocking collectives, body(): both = lax.all_gather(message, 'line', axis=0)  3.32 us
    ppermute x1, waiting for transfers between devices, body(): from_two = lax.ppermute(two, both_axes, ops[1])  3.07 us
    pallas_call x7, Pallas kernels, call(): pl.pallas_call(kernel, out_shape=outs, compiler_params=pltpu.CompilerPara...  1.71 us
    ppermute x1, starting transfers between devices, body(): from_one = lax.ppermute(one, both_axes, ops[0])  1.42 us
    ppermute x1, starting transfers between devices, body(): from_three = lax.ppermute(three, both_axes, ops[2])  1.3 us
  transfers between devices with their start and end apart: 3, of which 1 were waited for; matrix products, arithmetic and copies ran while one was open for 0% of the time, Pallas kernels for 4%

profile of v4, /device:TPU:257, one launch (start us, length us, event | category | flops | bytes accessed | tf_op | source)
XLA Modules:
  0.0 16.7 jit_solution(14115159542962408969)
XLA Ops:
  0.0 0.0 copy-start.1
  0.0 0.0 copy-start
  0.0 0.0 copy-start.2
  0.1 1.4 %collective-permute-start = (f32[24,8,128]{2,1,0:T(8,128)S(1)}, f32[24,8,128]{2,1,0:T(8,128)S(1)}, u32[]{:S(2)}, u32[]{:S(2)}) collective-permute-start(f32[24,8,128]{2,1,0:T(8,128)S(1)} %get-tuple-element.34), channel_id=1, source_target_pairs={{5,4},{9,8},{13,12},{17,16},{21,20},{25,24},{29,28},{33,32},{37,36... | collective-permute-start | bytes 294920 | tf_op jit(solution)/shard_map/ppermute | solution.py:493
  1.5 0.0 copy-done.2
  1.5 0.0 copy-done.1
  1.5 0.0 copy-done
  1.5 0.1 ends.1
  1.7 5.8 %collective-permute-start.1 = (f32[24,8,128]{2,1,0:T(8,128)S(1)}, f32[24,8,128]{2,1,0:T(8,128)S(1)}, u32[]{:S(2)}, u32[]{:S(2)}) collective-permute-start(f32[24,8,128]{2,1,0:T(8,128)S(1)} %get-tuple-element.35), channel_id=1, source_target_pairs={{3,4},{4,3},{5,6},{6,5},{7,8},{8,7},{9,10},{10,9},{11,12},{12,11},... | collective-permute-start | bytes 294920 | tf_op jit(solution)/shard_map/ppermute | solution.py:503
  7.4 0.0 collective-permute-done.arrived.one
  7.5 1.3 %collective-permute-start.2 = (f32[24,8,128]{2,1,0:T(8,128)S(1)}, f32[24,8,128]{2,1,0:T(8,128)S(1)}, u32[]{:S(2)}, u32[]{:S(2)}) collective-permute-start(f32[24,8,128]{2,1,0:T(8,128)S(1)} %third.1), channel_id=1, source_target_pairs={{2,3},{3,2},{6,7},{7,6},{4,5},{10,11},{11,10},{8,9},{14,15},{15,14... | collective-permute-start | bytes 294920 | tf_op jit(solution)/shard_map/ppermute | solution.py:505
  8.8 0.6 %local.1 = (f32[16,3,8,128]{3,2,1,0:T(8,128)S(1)}, f32[2,16,8,128]{3,2,1,0:T(8,128)S(1)}, f32[15,8,8,128]{3,2,1,0:T(8,128)S(1)}, f32[16,3,8,128]{3,2,1,0:T(8,128...) custom-call(f32[3,16,8,128]{3,2,1,0:T(8,128)S(1)} %get-tuple-element, ...), custom_call_target="tpu_custom_call" | custom-call | flops 8388608 | bytes 1048576 | tf_op jit(solution)/shard_map/local/pallas_call | solution.py:448
  9.4 3.1 %collective-permute-done.1.two = f32[24,8,128]{2,1,0:T(8,128)S(1)} collective-permute-done((f32[24,8,128]{2,1,0:T(8,128)S(1)}, f32[24,8,128]{2,1,0:T(8,128)S(1)}, u32[]{:S(2)}, u32[]{:S(2)}) %collective-permute-start.1) | collective-permute-done | bytes 98336 | tf_op jit(solution)/shard_map/ppermute | solution.py:503
  12.4 0.0 collective-permute-done.2.three
  12.4 0.3 %finish.1 = (f32[2,128,128]{2,1,0:T(8,128)S(1)}, f32[8,128]{1,0:T(8,128)S(1)}) custom-call(f32[16,3,8,128]{3,2,1,0:T(8,128)S(1)} %get-tuple-element.27.k_all, f32[2,16,8,128]{3,2,1,0:T(8,128)S(1)} %get-tuple-element.28.rhs, f32[3,16,8,128]{3,2,1,0:T(8,128)S(1)} %get-tuple-element.25.kept, f32[15,8,8,128]{3,2,1,0:T(8,128)S(1)} %get-tuple-element.29.ab, ...), custom_call_target="tpu_custom_call" | custom-call | flops 2097152 | bytes 1048576 | tf_op jit(solution)/shard_map/finish/pallas_call | solution.py:448
  12.7 3.3 %all-gather = f32[16,128]{1,0:T(8,128)S(1)} all-gather(f32[8,128]{1,0:T(8,128)S(1)} %get-tuple-element.38), channel_id=2, replica_groups=mesh['line'=2,'tile'=256] {'line'}, dimensions={0}, use_global_device_ids=true | all-gather | bytes 12288 | tf_op jit(solution)/shard_map/all_gather | solution.py:529
  16.0 0.7 %join.1 = f32[2,128,128]{2,1,0:T(8,128)} custom-call(f32[2,128,128]{2,1,0:T(8,128)S(1)} %get-tuple-element.36.local_x, f32[4,128,128]{2,1,0:T(8,128)S(1)} %get-tuple-element.37.answer, f32[2,8,128]{2,1,0:T(8,128)S(1)} %bitcast.1), custom_call_target="tpu_custom_call" | custom-call | flops 262144 | bytes 1048576 | tf_op jit(solution)/shard_map/join/pallas_call | solution.py:448
  (3 shorter events, 0.1 us)
Async XLA Ops:
  0.0 1.5 %copy-start.1 = (f32[128,128]{1,0:T(8,128)S(1)}, f32[128,128]{1,0:T(8,128)}, u32[]{:S(2)}) copy-start(f32[128,128]{1,0:T(8,128)} %sat.1) | copy-start | bytes 196612
  0.0 1.5 %copy-start = (f32[2,128,128]{2,1,0:T(8,128)S(1)}, f32[2,128,128]{2,1,0:T(8,128)}, u32[]{:S(2)}) copy-start(f32[2,128,128]{2,1,0:T(8,128)} %field.1) | copy-start | bytes 393220
  0.0 1.4 %copy-start.2 = (s32[1,128]{1,0:T(1,128)S(1)}, s32[1,128]{1,0:T(1,128)}, u32[]{:S(2)}) copy-start(s32[1,128]{1,0:T(1,128)} %mask_hbm.1) | copy-start | bytes 1540
  0.1 7.4 %collective-permute-start = (f32[24,8,128]{2,1,0:T(8,128)S(1)}, f32[24,8,128]{2,1,0:T(8,128)S(1)}, u32[]{:S(2)}, u32[]{:S(2)}) collective-permute-start(f32[24,8,128]{2,1,0:T(8,128)S(1)} %get-tuple-element.34), channel_id=1, source_target_pairs={{5,4},{9,8},{13,12},{17,16},{21,20},{25,24},{29,28},{33,32},{37,36... | collective-permute-start | bytes 294920 | tf_op jit(solution)/shard_map/ppermute | solution.py:493
  1.7 10.8 %collective-permute-start.1 = (f32[24,8,128]{2,1,0:T(8,128)S(1)}, f32[24,8,128]{2,1,0:T(8,128)S(1)}, u32[]{:S(2)}, u32[]{:S(2)}) collective-permute-start(f32[24,8,128]{2,1,0:T(8,128)S(1)} %get-tuple-element.35), channel_id=1, source_target_pairs={{3,4},{4,3},{5,6},{6,5},{7,8},{8,7},{9,10},{10,9},{11,12},{12,11},... | collective-permute-start | bytes 294920 | tf_op jit(solution)/shard_map/ppermute | solution.py:503
  7.5 4.9 %collective-permute-start.2 = (f32[24,8,128]{2,1,0:T(8,128)S(1)}, f32[24,8,128]{2,1,0:T(8,128)S(1)}, u32[]{:S(2)}, u32[]{:S(2)}) collective-permute-start(f32[24,8,128]{2,1,0:T(8,128)S(1)} %third.1), channel_id=1, source_target_pairs={{2,3},{3,2},{6,7},{7,6},{4,5},{10,11},{11,10},{8,9},{14,15},{15,14... | collective-permute-start | bytes 294920 | tf_op jit(solution)/shard_map/ppermute | solution.py:505

commit v5 on v4

--- a/solution.py
+++ b/solution.py
@@ -124,10 +124,9 @@
 def pack_even(kept, turned, even):
     near = toward_odd()
     half = STEPS // 2
-    for i in range(STEPS):
-        even[i] = jnp.where(near, turned[i], kept[0, i])
-    for i in range(half):
-        even[STEPS + i] = jnp.where(near, turned[STEPS + i], kept[2, i])
+    for j in range(3):
+        for i in range(half):
+            even[j * half + i] = jnp.where(near, turned[j * half + i], kept[j, i])
 
 
 def signs(mask, sign):
@@ -139,21 +138,13 @@
     half = STEPS // 2
     rows = [pl.ds(i, CHUNKS, stride=STEPS) for i in range(STEPS)]
     sign = sign[...]
-    for i in range(STEPS):
-        f1 = field[1, rows[i], :] * (1.0 / SCALE)
-        kept[1, i] = f1
-        turned[i] = roll(f1, XS, 1)
-    for i in range(STEPS):
-        s = sat[rows[i], :] * sign
-        kept[2, i] = s
-        if i >= half:
-            high = roll(s, XS, 1)
-            turned[STEPS + i - half] = high
-            odd[STEPS + i - half] = jnp.where(near, kept[2, i - half], high)
-    for i in range(STEPS):
-        f0 = field[0, rows[i], :]
-        kept[0, i] = f0
-        odd[i] = jnp.where(near, f0, turned[i])
+    for i in (*range(half, STEPS), *range(half)):
+        for j, x in enumerate((field[0, rows[i], :], field[1, rows[i], :] * (1.0 / SCALE), sat[rows[i], :] * sign)):
+            kept[j, i] = x
+            if i >= half:
+                turned[(j - 1) * half + i] = roll(x, XS, 1)
+            else:
+                odd[j * half + i] = jnp.where(near, x, turned[j * half + i])
 
 
 def tile():
@@ -214,13 +205,14 @@
             out[i] = arrived[i]
 
 
-def local(kept, turned, k_all, rhs, ab, dinv, ring, final, answer, share):
+def local(kept, turned, one, k_all, rhs, ab, dinv, ring, final, answer, share, own):
     first, last = chunks() == 0, chunks() == CHUNKS - 1
     low_line, high_line = line() == 0, line() == 1
     column = lax.rem(lanes(), XS)
     west_end, east_end = column == 0, column == XS - 1
     half = STEPS // 2
 
+    near = toward_odd()
     k = []
     for i in range(STEPS):
         s = kept[2, i]
@@ -228,9 +220,17 @@
         k.append(ki)
         store(k_all, (i,), ki)
         f = (kept[0, i], kept[1, i])
-        far = (roll(f[0], XS, 1), turned[i])
-        far_s = turned[STEPS + i - half] if i >= half else roll(s, XS, 1)
-        total = flux(add(ki, conduct(far_s)), (far[0] - f[0], far[1] - f[1]))
+        if i < half:
+            far, far_s = (roll(f[0], XS, 1), roll(f[1], XS, 1)), roll(s, XS, 1)
+        else:
+            far, far_s = (turned[i - half], turned[i]), turned[i + half]
+        far_k = conduct(far_s)
+        if i < half:
+            store(own, (i,), (*far_k, *far))
+        else:
+            held = load(own, i - half)
+            store(own, (i - half,), tuple(jnp.where(near, x, y) for x, y in zip((*ki, *f), held)))
+        total = flux(add(ki, far_k), (far[0] - f[0], far[1] - f[1]))
         west_k = conduct(roll(s, 1, 1))
         west = flux(add(ki, west_k), (roll(f[0], 1, 1) - f[0], roll(f[1], 1, 1) - f[1]))
         edge = flux(ki, f)
@@ -238,6 +238,15 @@
         east = tuple(jnp.where(east_end, e, roll(w, -1, 1)) for e, w in zip(edge, west))
         for j in range(2):
             rhs[j, i] = f[j] + (total[j] + (west[j] - east[j]))
+
+    @pl.when(from_first())
+    def _():
+        for i in range(STEPS):
+            pack = [one[j * half + i % half] for j in range(3)]
+            far = pack if i >= half else [roll(x, XS, 1) for x in pack]
+            total = flux(add(load(k_all, i), conduct(far[2])), (far[0] - kept[0, i], far[1] - kept[1, i]))
+            for j in range(2):
+                rhs[j, i] = rhs[j, i] + jnp.where(near, 0.0, total[j])
 
     upper = {i: wide(add(k[i], k[i + 1])) for i in range(STEPS - 1)}
     upper[STEPS - 1] = wide(tuple(jnp.where(last, 0.0, x) for x in add(k[-1], down(k[0], -1))))
@@ -337,18 +346,48 @@
     share[pl.ds(6, 2), :] = none[0:2]
 
 
-def finish(k_all, rhs, kept, ab, dinv, ring, final, share, one, two, three, local_x, message):
-    rest = (k_all, rhs, kept, ab, dinv, ring, final, share, local_x, message)
-
-    @pl.when(tile() >= ROW)
-    def _():
-        place = lax.rem(tile(), ROW)
-        solve(lambda i: (two[i], jnp.where(place == 0, one[i], three[i])), *rest)
-
-    @pl.when(tile() < ROW)
-    def _():
-        at, high = tile(), line() == 1
-
+def from_first():
+    return jnp.logical_and(tile() >= ROW, lax.rem(tile(), ROW) == 0)
+
+
+def finish(k_all, rhs, kept, own, ab, dinv, ring, final, share, one, two, three, local_x, message):
+    half = STEPS // 2
+    at, high = tile(), line() == 1
+    near = toward_odd()
+    rest = (ab, dinv, ring, final, share, local_x, message)
+
+    @pl.when(from_first())
+    def _():
+        b = {i: (rhs[0, i], rhs[1, i]) for i in range(STEPS)}
+        for i in range(half):
+            mine = load(own, i)
+            total = flux(add(mine[:3], conduct(two[2 * half + i])), (two[i] - mine[3], two[half + i] - mine[4]))
+            b[i + half] = add(b[i + half], tuple(jnp.where(near, x, 0.0) for x in total))
+            b[i] = add(b[i], tuple(jnp.where(near, roll(x, XS, 1), 0.0) for x in total))
+        solve(b, *rest)
+
+    def both(halo):
+        alone = jnp.logical_or(at == 0, at == lax.axis_size("tile") - 1)
+        inside = jnp.logical_not(jnp.logical_and(near, alone))
+        far = {}
+        for j in range(3):
+            for i in range(half):
+                o, e = halo(j * half + i)
+                far[j, i] = roll(jnp.where(near, e, o), XS, 1)
+                far[j, i + half] = jnp.where(near, o, e)
+        b = {}
+        for i in range(STEPS):
+            drop = (far[0, i] - kept[0, i], far[1, i] - kept[1, i])
+            total = flux(add(load(k_all, i), conduct(far[2, i], inside)), drop)
+            b[i] = (rhs[0, i] + total[0], rhs[1, i] + total[1])
+        solve(b, *rest)
+
+    @pl.when(jnp.logical_and(at >= ROW, jnp.logical_not(from_first())))
+    def _():
+        both(lambda i: (two[i], three[i]))
+
+    @pl.when(at < ROW)
+    def _():
         def halo(i):
             odd = jnp.where(at == 1, one[i], two[i])
             odd = jnp.where(jnp.logical_and(high, at == 2), one[i], odd)
@@ -356,28 +395,10 @@
             even = jnp.where(jnp.logical_or(at == 1, jnp.logical_and(high, at == 0)), two[i], three[i])
             return odd, even
 
-        solve(halo, *rest)
-
-
-def solve(halo, k_all, rhs, kept, ab, dinv, ring, final, share, local_x, message):
-    near = toward_odd()
-    alone = jnp.logical_or(tile() == 0, tile() == lax.axis_size("tile") - 1)
-    inside = jnp.logical_not(jnp.logical_and(near, alone))
-    half = STEPS // 2
-    far_s, far_0, far_1 = [None] * STEPS, [], []
-    for i in range(half):
-        o, e = halo(STEPS + i)
-        far_s[i] = roll(jnp.where(near, e, o), XS, 1)
-        far_s[i + half] = jnp.where(near, o, e)
-    for i in range(STEPS):
-        o, e = halo(i)
-        far_0.append(roll(jnp.where(near, e, o), XS, 1))
-        far_1.append(jnp.where(near, o, e))
-    b = {}
-    for i in range(STEPS):
-        drop = (far_0[i] - kept[0, i], far_1[i] - kept[1, i])
-        total = flux(add(load(k_all, i), conduct(far_s[i], inside)), drop)
-        b[i] = (rhs[0, i] + total[0], rhs[1, i] + total[1])
+        both(halo)
+
+
+def solve(b, ab, dinv, ring, final, share, local_x, message):
     for stride, keep, drop in levels():
         for i in keep:
             left = i - stride
@@ -503,7 +524,7 @@
     from_two = lax.ppermute(two, both_axes, ops[1])
     (three,) = call(third, [tiles(PACK)], (kept, turned, from_one), "third", 1 << 12)
     from_three = lax.ppermute(three, both_axes, ops[2])
-    k_all, rhs, ab, dinv, ring, final, answer, share = call(
+    k_all, rhs, ab, dinv, ring, final, answer, share, own = call(
         local,
         [
             tiles(STEPS, 3),
@@ -514,15 +535,16 @@
             tiles(3),
             jax.ShapeDtypeStruct((4, cells, LANES), jnp.float32),
             jax.ShapeDtypeStruct((8, LANES), jnp.float32),
+            tiles(STEPS // 2, 5),
         ],
-        (kept, turned),
+        (kept, turned, from_one),
         "local",
         1 << 23,
     )
     local_x, message = call(
         finish,
         [jax.ShapeDtypeStruct((2, cells, LANES), jnp.float32), jax.ShapeDtypeStruct((8, LANES), jnp.float32)],
-        (k_all, rhs, kept, ab, dinv, ring, final, share, from_one, from_two, from_three),
+        (k_all, rhs, kept, own, ab, dinv, ring, final, share, from_one, from_two, from_three),
         "finish",
         1 << 21,
     )

time: 16.9 us -> 16.8 us (level)
  transfers between devices with their start and end apart: 3 -> 3, of which waited for: 1 -> 1; matrix products, arithmetic and copies ran while one was open for 0% -> 0% of each run, Pallas kernels for 4% -> 5%
where the time goes in v5:
time: 16.8 us; the launch traced here: 16.7 us
  starting transfers between devices  8.51 us (51%)
  blocking collectives  3.32 us (20%)
  waiting for transfers between devices  2.94 us (18%)
  Pallas kernels  1.79 us (11%)
    ppermute x1, starting transfers between devices, body(): from_two = lax.ppermute(two, both_axes, ops[1])  5.79 us
    all_gather x1, blocking collectives, body(): both = lax.all_gather(message, 'line', axis=0)  3.32 us
    ppermute x1, waiting for transfers between devices, body(): from_two = lax.ppermute(two, both_axes, ops[1])  2.93 us
    pallas_call x7, Pallas kernels, call(): pl.pallas_call(kernel, out_shape=outs, compiler_params=pltpu.CompilerPara...  1.79 us
    ppermute x1, starting transfers between devices, body(): from_one = lax.ppermute(one, both_axes, ops[0])  1.42 us
    ppermute x1, starting transfers between devices, body(): from_three = lax.ppermute(three, both_axes, ops[2])  1.3 us
  transfers between devices with their start and end apart: 3, of which 1 were waited for; matrix products, arithmetic and copies ran while one was open for 0% of the time, Pallas kernels for 5%

profile of v5, /device:TPU:257, one launch (start us, length us, event | category | flops | bytes accessed | tf_op | source)
XLA Modules:
  0.0 16.7 jit_solution(15327782357237071520)
XLA Ops:
  0.0 0.0 copy-start.1
  0.0 0.0 copy-start
  0.0 0.0 copy-start.2
  0.1 1.4 %collective-permute-start = (f32[24,8,128]{2,1,0:T(8,128)S(1)}, f32[24,8,128]{2,1,0:T(8,128)S(1)}, u32[]{:S(2)}, u32[]{:S(2)}) collective-permute-start(f32[24,8,128]{2,1,0:T(8,128)S(1)} %get-tuple-element.28), channel_id=1, source_target_pairs={{5,4},{9,8},{13,12},{17,16},{21,20},{25,24},{29,28},{33,32},{37,36... | collective-permute-start | bytes 294920 | tf_op jit(solution)/shard_map/ppermute | solution.py:514
  1.5 0.0 copy-done.2
  1.5 0.0 copy-done.1
  1.5 0.0 copy-done
  1.5 0.1 ends.1
  1.7 5.8 %collective-permute-start.1 = (f32[24,8,128]{2,1,0:T(8,128)S(1)}, f32[24,8,128]{2,1,0:T(8,128)S(1)}, u32[]{:S(2)}, u32[]{:S(2)}) collective-permute-start(f32[24,8,128]{2,1,0:T(8,128)S(1)} %get-tuple-element.37), channel_id=1, source_target_pairs={{3,4},{4,3},{5,6},{6,5},{7,8},{8,7},{9,10},{10,9},{11,12},{12,11},... | collective-permute-start | bytes 294920 | tf_op jit(solution)/shard_map/ppermute | solution.py:524
  7.4 0.0 collective-permute-done.one.arrived
  7.5 1.3 %collective-permute-start.2 = (f32[24,8,128]{2,1,0:T(8,128)S(1)}, f32[24,8,128]{2,1,0:T(8,128)S(1)}, u32[]{:S(2)}, u32[]{:S(2)}) collective-permute-start(f32[24,8,128]{2,1,0:T(8,128)S(1)} %third.1), channel_id=1, source_target_pairs={{2,3},{3,2},{6,7},{7,6},{4,5},{10,11},{11,10},{8,9},{14,15},{15,14... | collective-permute-start | bytes 294920 | tf_op jit(solution)/shard_map/ppermute | solution.py:526
  8.8 0.7 %local.1 = (f32[16,3,8,128]{3,2,1,0:T(8,128)S(1)}, f32[2,16,8,128]{3,2,1,0:T(8,128)S(1)}, f32[15,8,8,128]{3,2,1,0:T(8,128)S(1)}, f32[16,3,8,128]{3,2,1,0:T(8,128...) custom-call(f32[3,16,8,128]{3,2,1,0:T(8,128)S(1)} %get-tuple-element, ...), custom_call_target="tpu_custom_call" | custom-call | flops 8388608 | bytes 1048576 | tf_op jit(solution)/shard_map/local/pallas_call | solution.py:469
  9.5 2.9 %collective-permute-done.1.two = f32[24,8,128]{2,1,0:T(8,128)S(1)} collective-permute-done((f32[24,8,128]{2,1,0:T(8,128)S(1)}, f32[24,8,128]{2,1,0:T(8,128)S(1)}, u32[]{:S(2)}, u32[]{:S(2)}) %collective-permute-start.1) | collective-permute-done | bytes 98336 | tf_op jit(solution)/shard_map/ppermute | solution.py:524
  12.4 0.0 collective-permute-done.2.three
  12.4 0.2 %finish.1 = (f32[2,128,128]{2,1,0:T(8,128)S(1)}, f32[8,128]{1,0:T(8,128)S(1)}) custom-call(f32[16,3,8,128]{3,2,1,0:T(8,128)S(1)} %get-tuple-element.29.k_all, f32[2,16,8,128]{3,2,1,0:T(8,128)S(1)} %get-tuple-element.30.rhs, f32[3,16,8,128]{3,2,1,0:T(8,128)S(1)} %get-tuple-element.26.kept, f32[8,5,8,128]{3,2,1,0:T(8,128)S(1)} %get-tuple-element.31.own, ...), custom_call_target="tpu_custom_call" | custom-call | flops 2097152 | bytes 1048576 | tf_op jit(solution)/shard_map/finish/pallas_call | solution.py:469
  12.7 3.3 %all-gather = f32[16,128]{1,0:T(8,128)S(1)} all-gather(f32[8,128]{1,0:T(8,128)S(1)} %get-tuple-element.40), channel_id=2, replica_groups=mesh['line'=2,'tile'=256] {'line'}, dimensions={0}, use_global_device_ids=true | all-gather | bytes 12288 | tf_op jit(solution)/shard_map/all_gather | solution.py:551
  16.0 0.7 %join.1 = f32[2,128,128]{2,1,0:T(8,128)} custom-call(f32[2,128,128]{2,1,0:T(8,128)S(1)} %get-tuple-element.38.local_x, f32[4,128,128]{2,1,0:T(8,128)S(1)} %get-tuple-element.39.answer, f32[2,8,128]{2,1,0:T(8,128)S(1)} %bitcast.1), custom_call_target="tpu_custom_call" | custom-call | flops 262144 | bytes 1048576 | tf_op jit(solution)/shard_map/join/pallas_call | solution.py:469
  (3 shorter events, 0.1 us)
Async XLA Ops:
  0.0 1.5 %copy-start.1 = (f32[128,128]{1,0:T(8,128)S(1)}, f32[128,128]{1,0:T(8,128)}, u32[]{:S(2)}) copy-start(f32[128,128]{1,0:T(8,128)} %sat.1) | copy-start | bytes 196612
  0.0 1.5 %copy-start = (f32[2,128,128]{2,1,0:T(8,128)S(1)}, f32[2,128,128]{2,1,0:T(8,128)}, u32[]{:S(2)}) copy-start(f32[2,128,128]{2,1,0:T(8,128)} %field.1) | copy-start | bytes 393220
  0.0 1.4 %copy-start.2 = (s32[1,128]{1,0:T(1,128)S(1)}, s32[1,128]{1,0:T(1,128)}, u32[]{:S(2)}) copy-start(s32[1,128]{1,0:T(1,128)} %mask_hbm.1) | copy-start | bytes 1540
  0.1 7.4 %collective-permute-start = (f32[24,8,128]{2,1,0:T(8,128)S(1)}, f32[24,8,128]{2,1,0:T(8,128)S(1)}, u32[]{:S(2)}, u32[]{:S(2)}) collective-permute-start(f32[24,8,128]{2,1,0:T(8,128)S(1)} %get-tuple-element.28), channel_id=1, source_target_pairs={{5,4},{9,8},{13,12},{17,16},{21,20},{25,24},{29,28},{33,32},{37,36... | collective-permute-start | bytes 294920 | tf_op jit(solution)/shard_map/ppermute | solution.py:514
  1.7 10.8 %collective-permute-start.1 = (f32[24,8,128]{2,1,0:T(8,128)S(1)}, f32[24,8,128]{2,1,0:T(8,128)S(1)}, u32[]{:S(2)}, u32[]{:S(2)}) collective-permute-start(f32[24,8,128]{2,1,0:T(8,128)S(1)} %get-tuple-element.37), channel_id=1, source_target_pairs={{3,4},{4,3},{5,6},{6,5},{7,8},{8,7},{9,10},{10,9},{11,12},{12,11},... | collective-permute-start | bytes 294920 | tf_op jit(solution)/shard_map/ppermute | solution.py:524
  7.5 4.9 %collective-permute-start.2 = (f32[24,8,128]{2,1,0:T(8,128)S(1)}, f32[24,8,128]{2,1,0:T(8,128)S(1)}, u32[]{:S(2)}, u32[]{:S(2)}) collective-permute-start(f32[24,8,128]{2,1,0:T(8,128)S(1)} %third.1), channel_id=1, source_target_pairs={{2,3},{3,2},{6,7},{7,6},{4,5},{10,11},{11,10},{8,9},{14,15},{15,14... | collective-permute-start | bytes 294920 | tf_op jit(solution)/shard_map/ppermute | solution.py:526

commit v6 on v5

--- a/solution.py
+++ b/solution.py
@@ -138,13 +138,18 @@
     half = STEPS // 2
     rows = [pl.ds(i, CHUNKS, stride=STEPS) for i in range(STEPS)]
     sign = sign[...]
+    low, high = [None] * PACK, [None] * PACK
     for i in (*range(half, STEPS), *range(half)):
-        for j, x in enumerate((field[0, rows[i], :], field[1, rows[i], :] * (1.0 / SCALE), sat[rows[i], :] * sign)):
+        for j, x in reversed(list(enumerate((field[0, rows[i], :], field[1, rows[i], :] * (1.0 / SCALE), sat[rows[i], :] * sign)))):
+            if i >= half:
+                high[(j - 1) * half + i] = roll(x, XS, 1)
+            else:
+                low[j * half + i] = x
             kept[j, i] = x
-            if i >= half:
-                turned[(j - 1) * half + i] = roll(x, XS, 1)
-            else:
-                odd[j * half + i] = jnp.where(near, x, turned[j * half + i])
+    for i in range(PACK):
+        odd[i] = jnp.where(near, low[i], high[i])
+    for i in range(PACK):
+        turned[i] = high[i]
 
 
 def tile():

time: 16.8 us -> 16.8 us (level)
  no operation moved by 1% of the time
where the time goes in v6:
time: 16.8 us; the launch traced here: 16.7 us
  starting transfers between devices  8.51 us (51%)
  blocking collectives  3.32 us (20%)
  waiting for transfers between devices  2.94 us (18%)
  Pallas kernels  1.79 us (11%)
    ppermute x1, starting transfers between devices, body(): from_two = lax.ppermute(two, both_axes, ops[1])  5.79 us
    all_gather x1, blocking collectives, body(): both = lax.all_gather(message, 'line', axis=0)  3.32 us
    ppermute x1, waiting for transfers between devices, body(): from_two = lax.ppermute(two, both_axes, ops[1])  2.93 us
    pallas_call x7, Pallas kernels, call(): pl.pallas_call(kernel, out_shape=outs, compiler_params=pltpu.CompilerPara...  1.79 us
    ppermute x1, starting transfers between devices, body(): from_one = lax.ppermute(one, both_axes, ops[0])  1.42 us
    ppermute x1, starting transfers between devices, body(): from_three = lax.ppermute(three, both_axes, ops[2])  1.3 us
  transfers between devices with their start and end apart: 3, of which 1 were waited for; matrix products, arithmetic and copies ran while one was open for 0% of the time, Pallas kernels for 5%

profile of v6, /device:TPU:257, one launch (start us, length us, event | category | flops | bytes accessed | tf_op | source)
XLA Modules:
  0.0 16.7 jit_solution(6950437669109718717)
XLA Ops:
  0.0 0.0 copy-start.1
  0.0 0.0 copy-start
  0.0 0.0 copy-start.2
  0.1 1.4 %collective-permute-start = (f32[24,8,128]{2,1,0:T(8,128)S(1)}, f32[24,8,128]{2,1,0:T(8,128)S(1)}, u32[]{:S(2)}, u32[]{:S(2)}) collective-permute-start(f32[24,8,128]{2,1,0:T(8,128)S(1)} %get-tuple-element.28), channel_id=1, source_target_pairs={{5,4},{9,8},{13,12},{17,16},{21,20},{25,24},{29,28},{33,32},{37,36... | collective-permute-start | bytes 294920 | tf_op jit(solution)/shard_map/ppermute | solution.py:519
  1.5 0.0 copy-done.2
  1.5 0.0 copy-done.1
  1.5 0.0 copy-done
  1.5 0.1 ends.1
  1.6 5.8 %collective-permute-start.1 = (f32[24,8,128]{2,1,0:T(8,128)S(1)}, f32[24,8,128]{2,1,0:T(8,128)S(1)}, u32[]{:S(2)}, u32[]{:S(2)}) collective-permute-start(f32[24,8,128]{2,1,0:T(8,128)S(1)} %get-tuple-element.37), channel_id=1, source_target_pairs={{3,4},{4,3},{5,6},{6,5},{7,8},{8,7},{9,10},{10,9},{11,12},{12,11},... | collective-permute-start | bytes 294920 | tf_op jit(solution)/shard_map/ppermute | solution.py:529
  7.4 0.0 collective-permute-done.one.arrived
  7.5 1.3 %collective-permute-start.2 = (f32[24,8,128]{2,1,0:T(8,128)S(1)}, f32[24,8,128]{2,1,0:T(8,128)S(1)}, u32[]{:S(2)}, u32[]{:S(2)}) collective-permute-start(f32[24,8,128]{2,1,0:T(8,128)S(1)} %third.1), channel_id=1, source_target_pairs={{2,3},{3,2},{6,7},{7,6},{4,5},{10,11},{11,10},{8,9},{14,15},{15,14... | collective-permute-start | bytes 294920 | tf_op jit(solution)/shard_map/ppermute | solution.py:531
  8.8 0.7 %local.1 = (f32[16,3,8,128]{3,2,1,0:T(8,128)S(1)}, f32[2,16,8,128]{3,2,1,0:T(8,128)S(1)}, f32[15,8,8,128]{3,2,1,0:T(8,128)S(1)}, f32[16,3,8,128]{3,2,1,0:T(8,128...) custom-call(f32[3,16,8,128]{3,2,1,0:T(8,128)S(1)} %get-tuple-element, ...), custom_call_target="tpu_custom_call" | custom-call | flops 8388608 | bytes 1048576 | tf_op jit(solution)/shard_map/local/pallas_call | solution.py:474
  9.5 2.9 %collective-permute-done.1.two = f32[24,8,128]{2,1,0:T(8,128)S(1)} collective-permute-done((f32[24,8,128]{2,1,0:T(8,128)S(1)}, f32[24,8,128]{2,1,0:T(8,128)S(1)}, u32[]{:S(2)}, u32[]{:S(2)}) %collective-permute-start.1) | collective-permute-done | bytes 98336 | tf_op jit(solution)/shard_map/ppermute | solution.py:529
  12.4 0.0 collective-permute-done.2.three
  12.4 0.2 %finish.1 = (f32[2,128,128]{2,1,0:T(8,128)S(1)}, f32[8,128]{1,0:T(8,128)S(1)}) custom-call(f32[16,3,8,128]{3,2,1,0:T(8,128)S(1)} %get-tuple-element.29.k_all, f32[2,16,8,128]{3,2,1,0:T(8,128)S(1)} %get-tuple-element.30.rhs, f32[3,16,8,128]{3,2,1,0:T(8,128)S(1)} %get-tuple-element.26.kept, f32[8,5,8,128]{3,2,1,0:T(8,128)S(1)} %get-tuple-element.31.own, ...), custom_call_target="tpu_custom_call" | custom-call | flops 2097152 | bytes 1048576 | tf_op jit(solution)/shard_map/finish/pallas_call | solution.py:474
  12.7 3.3 %all-gather = f32[16,128]{1,0:T(8,128)S(1)} all-gather(f32[8,128]{1,0:T(8,128)S(1)} %get-tuple-element.40), channel_id=2, replica_groups=mesh['line'=2,'tile'=256] {'line'}, dimensions={0}, use_global_device_ids=true | all-gather | bytes 12288 | tf_op jit(solution)/shard_map/all_gather | solution.py:556
  16.0 0.7 %join.1 = f32[2,128,128]{2,1,0:T(8,128)} custom-call(f32[2,128,128]{2,1,0:T(8,128)S(1)} %get-tuple-element.38.local_x, f32[4,128,128]{2,1,0:T(8,128)S(1)} %get-tuple-element.39.answer, f32[2,8,128]{2,1,0:T(8,128)S(1)} %bitcast.1), custom_call_target="tpu_custom_call" | custom-call | flops 262144 | bytes 1048576 | tf_op jit(solution)/shard_map/join/pallas_call | solution.py:474
  (3 shorter events, 0.1 us)
Async XLA Ops:
  0.0 1.5 %copy-start.1 = (f32[128,128]{1,0:T(8,128)S(1)}, f32[128,128]{1,0:T(8,128)}, u32[]{:S(2)}) copy-start(f32[128,128]{1,0:T(8,128)} %sat.1) | copy-start | bytes 196612
  0.0 1.5 %copy-start = (f32[2,128,128]{2,1,0:T(8,128)S(1)}, f32[2,128,128]{2,1,0:T(8,128)}, u32[]{:S(2)}) copy-start(f32[2,128,128]{2,1,0:T(8,128)} %field.1) | copy-start | bytes 393220
  0.0 1.4 %copy-start.2 = (s32[1,128]{1,0:T(1,128)S(1)}, s32[1,128]{1,0:T(1,128)}, u32[]{:S(2)}) copy-start(s32[1,128]{1,0:T(1,128)} %mask_hbm.1) | copy-start | bytes 1540
  0.1 7.4 %collective-permute-start = (f32[24,8,128]{2,1,0:T(8,128)S(1)}, f32[24,8,128]{2,1,0:T(8,128)S(1)}, u32[]{:S(2)}, u32[]{:S(2)}) collective-permute-start(f32[24,8,128]{2,1,0:T(8,128)S(1)} %get-tuple-element.28), channel_id=1, source_target_pairs={{5,4},{9,8},{13,12},{17,16},{21,20},{25,24},{29,28},{33,32},{37,36... | collective-permute-start | bytes 294920 | tf_op jit(solution)/shard_map/ppermute | solution.py:519
  1.6 10.8 %collective-permute-start.1 = (f32[24,8,128]{2,1,0:T(8,128)S(1)}, f32[24,8,128]{2,1,0:T(8,128)S(1)}, u32[]{:S(2)}, u32[]{:S(2)}) collective-permute-start(f32[24,8,128]{2,1,0:T(8,128)S(1)} %get-tuple-element.37), channel_id=1, source_target_pairs={{3,4},{4,3},{5,6},{6,5},{7,8},{8,7},{9,10},{10,9},{11,12},{12,11},... | collective-permute-start | bytes 294920 | tf_op jit(solution)/shard_map/ppermute | solution.py:529
  7.5 4.9 %collective-permute-start.2 = (f32[24,8,128]{2,1,0:T(8,128)S(1)}, f32[24,8,128]{2,1,0:T(8,128)S(1)}, u32[]{:S(2)}, u32[]{:S(2)}) collective-permute-start(f32[24,8,128]{2,1,0:T(8,128)S(1)} %third.1), channel_id=1, source_target_pairs={{2,3},{3,2},{6,7},{7,6},{4,5},{10,11},{11,10},{8,9},{14,15},{15,14... | collective-permute-start | bytes 294920 | tf_op jit(solution)/shard_map/ppermute | solution.py:531

commit v7 on v6

--- a/solution.py
+++ b/solution.py
@@ -210,7 +210,7 @@
             out[i] = arrived[i]
 
 
-def local(kept, turned, one, k_all, rhs, ab, dinv, ring, final, answer, share, own):
+def local(kept, turned, one, k_all, rhs, ab, dinv, ring, final, answer, share, own, green):
     first, last = chunks() == 0, chunks() == CHUNKS - 1
     low_line, high_line = line() == 0, line() == 1
     column = lax.rem(lanes(), XS)
@@ -340,6 +340,7 @@
             if i in sides:
                 w[i] = add(w[i], mul(wide(load(dinv, i)), sides[i]))
     for i in range(STEPS):
+        store(green, (i,), w[i])
         for j, x in enumerate((w[i][0], w[i][1], SCALE * w[i][2], SCALE * w[i][3])):
             answer[j, pl.ds(i, CHUNKS, stride=STEPS), :] = x
 
@@ -355,11 +356,11 @@
     return jnp.logical_and(tile() >= ROW, lax.rem(tile(), ROW) == 0)
 
 
-def finish(k_all, rhs, kept, own, ab, dinv, ring, final, share, one, two, three, local_x, message):
+def finish(k_all, rhs, kept, own, ab, dinv, ring, final, share, green, one, two, three, local_x, message, pending):
     half = STEPS // 2
     at, high = tile(), line() == 1
     near = toward_odd()
-    rest = (ab, dinv, ring, final, share, local_x, message)
+    rest = (ab, dinv, ring, final, share, green, local_x, message, pending)
 
     @pl.when(from_first())
     def _():
@@ -369,7 +370,7 @@
             total = flux(add(mine[:3], conduct(two[2 * half + i])), (two[i] - mine[3], two[half + i] - mine[4]))
             b[i + half] = add(b[i + half], tuple(jnp.where(near, x, 0.0) for x in total))
             b[i] = add(b[i], tuple(jnp.where(near, roll(x, XS, 1), 0.0) for x in total))
-        solve(b, *rest)
+        conclude(b, *rest)
 
     def both(halo):
         alone = jnp.logical_or(at == 0, at == lax.axis_size("tile") - 1)
@@ -385,7 +386,7 @@
             drop = (far[0, i] - kept[0, i], far[1, i] - kept[1, i])
             total = flux(add(load(k_all, i), conduct(far[2, i], inside)), drop)
             b[i] = (rhs[0, i] + total[0], rhs[1, i] + total[1])
-        solve(b, *rest)
+        conclude(b, *rest)
 
     @pl.when(jnp.logical_and(at >= ROW, jnp.logical_not(from_first())))
     def _():
@@ -403,7 +404,37 @@
         both(halo)
 
 
-def solve(b, ab, dinv, ring, final, share, local_x, message):
+def conclude(b, ab, dinv, ring, final, share, green, local_x, message, pending):
+    message[...] = share[...]
+
+    @pl.when(line() == 0)
+    def _():
+        parts = []
+        for i in range(STEPS):
+            w = load(green, i)
+            parts.append((w[0] * b[i][0] + w[2] * b[i][1], w[1] * b[i][0] + w[3] * b[i][1]))
+            store(pending, (i,), b[i])
+        while len(parts) > 1:
+            parts = [add(x, y) for x, y in zip(parts[::2], parts[1::2])]
+        d = parts[0]
+        for shift in (4, 2, 1):
+            d = add(d, down(d, shift))
+        for j in range(2):
+            message[pl.ds(j, 1), :] = d[j][0:1]
+
+    @pl.when(line() == 1)
+    def _():
+        x = solve(b, ab, dinv, ring, final)
+        for j in range(2):
+            message[pl.ds(j, 1), :] = x[0][j][0:1]
+        for i in range(STEPS):
+            here = pl.ds(i, CHUNKS, stride=STEPS)
+            local_x[0, here, :] = x[i][0]
+            local_x[1, here, :] = SCALE * x[i][1]
+
+
+def solve(b, ab, dinv, ring, final):
+    b = dict(b)
     for stride, keep, drop in levels():
         for i in keep:
             left = i - stride
@@ -427,17 +458,10 @@
             else:
                 after, later = turn(down(load(ab, PLACE[stride, 0])[0:4], -1)), down(x[0], -1)
             x[i] = add(apply(wide(load(dinv, i)), b[i]), apply(prev, x[left]), apply(after, later))
-    message[...] = share[...]
-    tail = down(x[STEPS - 1], 1)
-    for j in range(2):
-        message[pl.ds(j, 1), :] = jnp.where(line() == 0, tail[j], x[0][j])[0:1]
-    for i in range(STEPS):
-        here = pl.ds(i, CHUNKS, stride=STEPS)
-        local_x[0, here, :] = x[i][0]
-        local_x[1, here, :] = SCALE * x[i][1]
-
-
-def join(local_x, answer, both, out_hbm, out, sems):
+    return x
+
+
+def join(local_x, answer, both, pending, ab, dinv, ring, final, out_hbm, out, sems):
     def row(who, j):
         return jnp.broadcast_to(both[who, pl.ds(j, 1), :], TILE)
 
@@ -452,12 +476,29 @@
     through = ((m[3] * push[0] - m[1] * push[1]) * scale, (m[0] * push[1] - m[2] * push[0]) * scale)
 
     copies = [pltpu.make_async_copy(out.at[j], out_hbm.at[j], sems.at[j]) for j in range(2)]
-    for j in range(2):
+
+    @pl.when(line() == 0)
+    def _():
+        b = {i: load(pending, i) for i in range(STEPS)}
+        last = chunks() == CHUNKS - 1
+        b[STEPS - 1] = add(b[STEPS - 1], tuple(jnp.where(last, x, 0.0) for x in through))
+        x = solve(b, ab, dinv, ring, final)
         for i in range(STEPS):
-            here = pl.ds(i * CHUNKS, CHUNKS)
-            change = answer[2 * j, here, :] * through[0] + answer[2 * j + 1, here, :] * through[1]
-            out[j, here, :] = local_x[j, here, :] + change
-        copies[j].start()
+            here = pl.ds(i, CHUNKS, stride=STEPS)
+            out[0, here, :] = x[i][0]
+            out[1, here, :] = SCALE * x[i][1]
+        for copy in copies:
+            copy.start()
+
+    @pl.when(line() == 1)
+    def _():
+        for j in range(2):
+            for i in range(STEPS):
+                here = pl.ds(i * CHUNKS, CHUNKS)
+                change = answer[2 * j, here, :] * through[0] + answer[2 * j + 1, here, :] * through[1]
+                out[j, here, :] = local_x[j, here, :] + change
+            copies[j].start()
+
     for copy in copies:
         copy.wait()
 
@@ -529,7 +570,7 @@
     from_two = lax.ppermute(two, both_axes, ops[1])
     (three,) = call(third, [tiles(PACK)], (kept, turned, from_one), "third", 1 << 12)
     from_three = lax.ppermute(three, both_axes, ops[2])
-    k_all, rhs, ab, dinv, ring, final, answer, share, own = call(
+    k_all, rhs, ab, dinv, ring, final, answer, share, own, green = call(
         local,
         [
             tiles(STEPS, 3),
@@ -541,15 +582,16 @@
             jax.ShapeDtypeStruct((4, cells, LANES), jnp.float32),
             jax.ShapeDtypeStruct((8, LANES), jnp.float32),
             tiles(STEPS // 2, 5),
+            tiles(STEPS, 4),
         ],
         (kept, turned, from_one),
         "local",
         1 << 23,
     )
-    local_x, message = call(
+    local_x, message, pending = call(
         finish,
-        [jax.ShapeDtypeStruct((2, cells, LANES), jnp.float32), jax.ShapeDtypeStruct((8, LANES), jnp.float32)],
-        (k_all, rhs, kept, own, ab, dinv, ring, final, share, from_one, from_two, from_three),
+        [jax.ShapeDtypeStruct((2, cells, LANES), jnp.float32), jax.ShapeDtypeStruct((8, LANES), jnp.float32), tiles(STEPS, 2)],
+        (k_all, rhs, kept, own, ab, dinv, ring, final, share, green, from_one, from_two, from_three),
         "finish",
         1 << 21,
     )
@@ -557,7 +599,7 @@
     return call(
         join,
         jax.ShapeDtypeStruct((2, cells, LANES), jnp.float32),
-        (local_x, answer, both),
+        (local_x, answer, both, pending, ab, dinv, ring, final),
         "join",
         1 << 18,
         out_specs=pl.BlockSpec(memory_space=pltpu.HBM),

time: 16.8 us -> 16.8 us (level)
  no operation moved by 1% of the time
where the time goes in v7:
time: 16.8 us; the launch traced here: 16.6 us
  starting transfers between devices  8.51 us (51%)
  blocking collectives  3.23 us (19%)
  waiting for transfers between devices  2.92 us (17%)
  Pallas kernels  1.84 us (11%)
    ppermute x1, starting transfers between devices, body(): from_two = lax.ppermute(two, both_axes, ops[1])  5.79 us
    all_gather x1, blocking collectives, body(): both = lax.all_gather(message, 'line', axis=0)  3.23 us
    ppermute x1, waiting for transfers between devices, body(): from_two = lax.ppermute(two, both_axes, ops[1])  2.91 us
    pallas_call x7, Pallas kernels, call(): pl.pallas_call(kernel, out_shape=outs, compiler_params=pltpu.CompilerPara...  1.84 us
    ppermute x1, starting transfers between devices, body(): from_one = lax.ppermute(one, both_axes, ops[0])  1.42 us
    ppermute x1, starting transfers between devices, body(): from_three = lax.ppermute(three, both_axes, ops[2])  1.3 us
  transfers between devices with their start and end apart: 3, of which 1 were waited for; matrix products, arithmetic and copies ran while one was open for 0% of the time, Pallas kernels for 5%

profile of v7, /device:TPU:257, one launch (start us, length us, event | category | flops | bytes accessed | tf_op | source)
XLA Modules:
  0.0 16.6 jit_solution(9357279586552725606)
XLA Ops:
  0.0 0.0 copy-start.1
  0.0 0.0 copy-start
  0.0 0.0 copy-start.2
  0.1 1.4 %collective-permute-start = (f32[24,8,128]{2,1,0:T(8,128)S(1)}, f32[24,8,128]{2,1,0:T(8,128)S(1)}, u32[]{:S(2)}, u32[]{:S(2)}) collective-permute-start(f32[24,8,128]{2,1,0:T(8,128)S(1)} %get-tuple-element.30), channel_id=1, source_target_pairs={{5,4},{9,8},{13,12},{17,16},{21,20},{25,24},{29,28},{33,32},{37,36... | collective-permute-start | bytes 294920 | tf_op jit(solution)/shard_map/ppermute | solution.py:560
  1.5 0.0 copy-done.2
  1.5 0.0 copy-done.1
  1.5 0.0 copy-done
  1.5 0.1 ends.1
  1.6 5.8 %collective-permute-start.1 = (f32[24,8,128]{2,1,0:T(8,128)S(1)}, f32[24,8,128]{2,1,0:T(8,128)S(1)}, u32[]{:S(2)}, u32[]{:S(2)}) collective-permute-start(f32[24,8,128]{2,1,0:T(8,128)S(1)} %get-tuple-element.40), channel_id=1, source_target_pairs={{3,4},{4,3},{5,6},{6,5},{7,8},{8,7},{9,10},{10,9},{11,12},{12,11},... | collective-permute-start | bytes 294920 | tf_op jit(solution)/shard_map/ppermute | solution.py:570
  7.4 0.0 collective-permute-done.one.arrived
  7.5 1.3 %collective-permute-start.2 = (f32[24,8,128]{2,1,0:T(8,128)S(1)}, f32[24,8,128]{2,1,0:T(8,128)S(1)}, u32[]{:S(2)}, u32[]{:S(2)}) collective-permute-start(f32[24,8,128]{2,1,0:T(8,128)S(1)} %third.1), channel_id=1, source_target_pairs={{2,3},{3,2},{6,7},{7,6},{4,5},{10,11},{11,10},{8,9},{14,15},{15,14... | collective-permute-start | bytes 294920 | tf_op jit(solution)/shard_map/ppermute | solution.py:572
  8.8 0.7 %local.1 = (f32[16,3,8,128]{3,2,1,0:T(8,128)S(1)}, f32[2,16,8,128]{3,2,1,0:T(8,128)S(1)}, f32[15,8,8,128]{3,2,1,0:T(8,128)S(1)}, f32[16,3,8,128]{3,2,1,0:T(8,128...) custom-call(f32[3,16,8,128]{3,2,1,0:T(8,128)S(1)} %get-tuple-element, ...), custom_call_target="tpu_custom_call" | custom-call | flops 8388608 | bytes 1048576 | tf_op jit(solution)/shard_map/local/pallas_call | solution.py:515
  9.5 2.9 %collective-permute-done.1.two = f32[24,8,128]{2,1,0:T(8,128)S(1)} collective-permute-done((f32[24,8,128]{2,1,0:T(8,128)S(1)}, f32[24,8,128]{2,1,0:T(8,128)S(1)}, u32[]{:S(2)}, u32[]{:S(2)}) %collective-permute-start.1) | collective-permute-done | bytes 98336 | tf_op jit(solution)/shard_map/ppermute | solution.py:570
  12.4 0.0 collective-permute-done.2.three
  12.4 0.2 %finish.1 = (f32[2,128,128]{2,1,0:T(8,128)S(1)}, f32[8,128]{1,0:T(8,128)S(1)}, f32[16,2,8,128]{3,2,1,0:T(8,128)S(1)}) custom-call(f32[16,3,8,128]{3,2,1,0:T(8,128)S(1)} %get-tuple-element.31.k_all, f32[2,16,8,128]{3,2,1,0:T(8,128)S(1)} %get-tuple-element.32.rhs, f32[3,16,8,128]{3,2,1,0:T(8,128)S(1)} %get-tuple-element.28.kept, ...), custom_call_target="tpu_custom_call" | custom-call | flops 2097152 | bytes 1048576 | tf_op jit(solution)/shard_map/finish/pallas_call | solution.py:515
  12.7 3.2 %all-gather = f32[16,128]{1,0:T(8,128)S(1)} all-gather(f32[8,128]{1,0:T(8,128)S(1)} %get-tuple-element.43), channel_id=2, replica_groups=mesh['line'=2,'tile'=256] {'line'}, dimensions={0}, use_global_device_ids=true | all-gather | bytes 12288 | tf_op jit(solution)/shard_map/all_gather | solution.py:598
  15.9 0.7 %join.1 = f32[2,128,128]{2,1,0:T(8,128)} custom-call(f32[2,128,128]{2,1,0:T(8,128)S(1)} %get-tuple-element.41.local_x, f32[4,128,128]{2,1,0:T(8,128)S(1)} %get-tuple-element.42.answer, f32[2,8,128]{2,1,0:T(8,128)S(1)} %bitcast.1, f32[16,2,8,128]{3,2,1,0:T(8,128)S(1)} %get-tuple-element.44.pending, f32[15,8,8,128]{3,2,1,0:T(8,128)S(1)} %get-tuple-element.34.ab, ...), custom_call_target="tpu_custom_call" | custom-call | flops 262144 | bytes 1048576 | tf_op jit(solution)/shard_map/join/pallas_call | solution.py:515
  (3 shorter events, 0.1 us)
Async XLA Ops:
  0.0 1.5 %copy-start.1 = (f32[128,128]{1,0:T(8,128)S(1)}, f32[128,128]{1,0:T(8,128)}, u32[]{:S(2)}) copy-start(f32[128,128]{1,0:T(8,128)} %sat.1) | copy-start | bytes 196612
  0.0 1.5 %copy-start = (f32[2,128,128]{2,1,0:T(8,128)S(1)}, f32[2,128,128]{2,1,0:T(8,128)}, u32[]{:S(2)}) copy-start(f32[2,128,128]{2,1,0:T(8,128)} %field.1) | copy-start | bytes 393220
  0.0 1.4 %copy-start.2 = (s32[1,128]{1,0:T(1,128)S(1)}, s32[1,128]{1,0:T(1,128)}, u32[]{:S(2)}) copy-start(s32[1,128]{1,0:T(1,128)} %mask_hbm.1) | copy-start | bytes 1540
  0.1 7.4 %collective-permute-start = (f32[24,8,128]{2,1,0:T(8,128)S(1)}, f32[24,8,128]{2,1,0:T(8,128)S(1)}, u32[]{:S(2)}, u32[]{:S(2)}) collective-permute-start(f32[24,8,128]{2,1,0:T(8,128)S(1)} %get-tuple-element.30), channel_id=1, source_target_pairs={{5,4},{9,8},{13,12},{17,16},{21,20},{25,24},{29,28},{33,32},{37,36... | collective-permute-start | bytes 294920 | tf_op jit(solution)/shard_map/ppermute | solution.py:560
  1.6 10.8 %collective-permute-start.1 = (f32[24,8,128]{2,1,0:T(8,128)S(1)}, f32[24,8,128]{2,1,0:T(8,128)S(1)}, u32[]{:S(2)}, u32[]{:S(2)}) collective-permute-start(f32[24,8,128]{2,1,0:T(8,128)S(1)} %get-tuple-element.40), channel_id=1, source_target_pairs={{3,4},{4,3},{5,6},{6,5},{7,8},{8,7},{9,10},{10,9},{11,12},{12,11},... | collective-permute-start | bytes 294920 | tf_op jit(solution)/shard_map/ppermute | solution.py:570
  7.5 4.9 %collective-permute-start.2 = (f32[24,8,128]{2,1,0:T(8,128)S(1)}, f32[24,8,128]{2,1,0:T(8,128)S(1)}, u32[]{:S(2)}, u32[]{:S(2)}) collective-permute-start(f32[24,8,128]{2,1,0:T(8,128)S(1)} %third.1), channel_id=1, source_target_pairs={{2,3},{3,2},{6,7},{7,6},{4,5},{10,11},{11,10},{8,9},{14,15},{15,14... | collective-permute-start | bytes 294920 | tf_op jit(solution)/shard_map/ppermute | solution.py:572

commit v8 on v7

--- a/solution.py
+++ b/solution.py
@@ -78,6 +78,12 @@
 
 def down(items, shift):
     return tuple(roll(x, shift, 0) for x in items)
+
+
+def over_chunks(items):
+    for shift in (4, 2, 1):
+        items = add(items, down(items, shift))
+    return items
 
 
 def lanes():
@@ -210,7 +216,7 @@
             out[i] = arrived[i]
 
 
-def local(kept, turned, one, k_all, rhs, ab, dinv, ring, final, answer, share, own, green):
+def local(kept, turned, one, k_all, rhs, ab, dinv, ring, final, answer, share, own, green, own_green, known):
     first, last = chunks() == 0, chunks() == CHUNKS - 1
     low_line, high_line = line() == 0, line() == 1
     column = lax.rem(lanes(), XS)
@@ -344,6 +350,15 @@
         for j, x in enumerate((w[i][0], w[i][1], SCALE * w[i][2], SCALE * w[i][3])):
             answer[j, pl.ds(i, CHUNKS, stride=STEPS), :] = x
 
+    @pl.when(from_first())
+    def _():
+        total = apply(turn(w[0]), (rhs[0, 0], rhs[1, 0]))
+        for i in range(1, STEPS):
+            total = add(total, apply(turn(w[i]), (rhs[0, i], rhs[1, i])))
+        store(known, (), over_chunks(total))
+        for i in range(half):
+            store(own_green, (i,), tuple(jnp.where(near, x, roll(y, XS, 1)) for x, y in zip(w[i + half], w[i])))
+
     tail = down((w[STEPS - 1][0], w[STEPS - 1][1], w[STEPS - 1][3], kept[2, STEPS - 1]), 1)
     head = (w[0][0], w[0][1], w[0][3], kept[2, 0])
     for j, (x, y) in enumerate(zip(head, tail)):
@@ -356,7 +371,7 @@
     return jnp.logical_and(tile() >= ROW, lax.rem(tile(), ROW) == 0)
 
 
-def finish(k_all, rhs, kept, own, ab, dinv, ring, final, share, green, one, two, three, local_x, message, pending):
+def finish(k_all, rhs, kept, own, ab, dinv, ring, final, share, green, own_green, known, one, two, three, local_x, message, pending):
     half = STEPS // 2
     at, high = tile(), line() == 1
     near = toward_odd()
@@ -364,13 +379,32 @@
 
     @pl.when(from_first())
     def _():
-        b = {i: (rhs[0, i], rhs[1, i]) for i in range(STEPS)}
+        through = []
         for i in range(half):
             mine = load(own, i)
-            total = flux(add(mine[:3], conduct(two[2 * half + i])), (two[i] - mine[3], two[half + i] - mine[4]))
-            b[i + half] = add(b[i + half], tuple(jnp.where(near, x, 0.0) for x in total))
-            b[i] = add(b[i], tuple(jnp.where(near, roll(x, XS, 1), 0.0) for x in total))
-        conclude(b, *rest)
+            drop = (two[i] - mine[3], two[half + i] - mine[4])
+            through.append(flux(add(mine[:3], conduct(two[2 * half + i])), drop))
+
+        @pl.when(line() == 0)
+        def _():
+            parts = [apply(turn(load(own_green, i)), through[i]) for i in range(half)]
+            while len(parts) > 1:
+                parts = [add(x, y) for x, y in zip(parts[::2], parts[1::2])]
+            d = over_chunks(parts[0])
+            message[...] = share[...]
+            for j in range(2):
+                x = known[j] + jnp.where(near, d[j] + roll(d[j], XS, 1), 0.0)
+                message[pl.ds(j, 1), :] = x[0:1]
+            for i in range(half):
+                store(pending, (i,), through[i])
+
+        @pl.when(line() == 1)
+        def _():
+            b = {}
+            for i in range(half):
+                b[i + half] = tuple(rhs[j, i + half] + jnp.where(near, through[i][j], 0.0) for j in range(2))
+                b[i] = tuple(rhs[j, i] + jnp.where(near, roll(through[i][j], XS, 1), 0.0) for j in range(2))
+            conclude(b, *rest)
 
     def both(halo):
         alone = jnp.logical_or(at == 0, at == lax.axis_size("tile") - 1)
@@ -416,9 +450,7 @@
             store(pending, (i,), b[i])
         while len(parts) > 1:
             parts = [add(x, y) for x, y in zip(parts[::2], parts[1::2])]
-        d = parts[0]
-        for shift in (4, 2, 1):
-            d = add(d, down(d, shift))
+        d = over_chunks(parts[0])
         for j in range(2):
             message[pl.ds(j, 1), :] = d[j][0:1]
 
@@ -461,7 +493,7 @@
     return x
 
 
-def join(local_x, answer, both, pending, ab, dinv, ring, final, out_hbm, out, sems):
+def join(local_x, answer, both, rhs, pending, ab, dinv, ring, final, out_hbm, out, sems):
     def row(who, j):
         return jnp.broadcast_to(both[who, pl.ds(j, 1), :], TILE)
 
@@ -479,7 +511,16 @@
 
     @pl.when(line() == 0)
     def _():
-        b = {i: load(pending, i) for i in range(STEPS)}
+        half = STEPS // 2
+        near = toward_odd()
+        packed = from_first()
+        b = {}
+        for i in range(half):
+            low, high = load(pending, i), load(pending, i + half)
+            for step, left, flow in ((i, low, tuple(roll(x, XS, 1) for x in low)), (i + half, high, low)):
+                b[step] = tuple(
+                    jnp.where(packed, rhs[j, step] + jnp.where(near, flow[j], 0.0), left[j]) for j in range(2)
+                )
         last = chunks() == CHUNKS - 1
         b[STEPS - 1] = add(b[STEPS - 1], tuple(jnp.where(last, x, 0.0) for x in through))
         x = solve(b, ab, dinv, ring, final)
@@ -570,7 +611,7 @@
     from_two = lax.ppermute(two, both_axes, ops[1])
     (three,) = call(third, [tiles(PACK)], (kept, turned, from_one), "third", 1 << 12)
     from_three = lax.ppermute(three, both_axes, ops[2])
-    k_all, rhs, ab, dinv, ring, final, answer, share, own, green = call(
+    k_all, rhs, ab, dinv, ring, final, answer, share, own, green, own_green, known = call(
         local,
         [
             tiles(STEPS, 3),
@@ -583,6 +624,8 @@
             jax.ShapeDtypeStruct((8, LANES), jnp.float32),
             tiles(STEPS // 2, 5),
             tiles(STEPS, 4),
+            tiles(STEPS // 2, 4),
+            tiles(2),
         ],
         (kept, turned, from_one),
         "local",
@@ -591,7 +634,7 @@
     local_x, message, pending = call(
         finish,
         [jax.ShapeDtypeStruct((2, cells, LANES), jnp.float32), jax.ShapeDtypeStruct((8, LANES), jnp.float32), tiles(STEPS, 2)],
-        (k_all, rhs, kept, own, ab, dinv, ring, final, share, green, from_one, from_two, from_three),
+        (k_all, rhs, kept, own, ab, dinv, ring, final, share, green, own_green, known, from_one, from_two, from_three),
         "finish",
         1 << 21,
     )
@@ -599,7 +642,7 @@
     return call(
         join,
         jax.ShapeDtypeStruct((2, cells, LANES), jnp.float32),
-        (local_x, answer, both, pending, ab, dinv, ring, final),
+        (local_x, answer, both, rhs, pending, ab, dinv, ring, final),
         "join",
         1 << 18,
         out_specs=pl.BlockSpec(memory_space=pltpu.HBM),

time: 16.8 us -> 16.7 us (level)
  transfers between devices with their start and end apart: 3 -> 3, of which waited for: 1 -> 1; matrix products, arithmetic and copies ran while one was open for 0% -> 0% of each run, Pallas kernels for 5% -> 6%
where the time goes in v8:
time: 16.7 us; the launch traced here: 16.6 us
  starting transfers between devices  8.51 us (51%)
  blocking collectives  3.18 us (19%)
  waiting for transfers between devices  2.82 us (17%)
  Pallas kernels  1.95 us (12%)
    ppermute x1, starting transfers between devices, body(): from_two = lax.ppermute(two, both_axes, ops[1])  5.79 us
    all_gather x1, blocking collectives, body(): both = lax.all_gather(message, 'line', axis=0)  3.18 us
    ppermute x1, waiting for transfers between devices, body(): from_two = lax.ppermute(two, both_axes, ops[1])  2.81 us
    pallas_call x7, Pallas kernels, call(): pl.pallas_call(kernel, out_shape=outs, compiler_params=pltpu.CompilerPara...  1.95 us
    ppermute x1, starting transfers between devices, body(): from_one = lax.ppermute(one, both_axes, ops[0])  1.42 us
    ppermute x1, starting transfers between devices, body(): from_three = lax.ppermute(three, both_axes, ops[2])  1.3 us
  transfers between devices with their start and end apart: 3, of which 1 were waited for; matrix products, arithmetic and copies ran while one was open for 0% of the time, Pallas kernels for 6%

profile of v8, /device:TPU:257, one launch (start us, length us, event | category | flops | bytes accessed | tf_op | source)
XLA Modules:
  0.0 16.6 jit_solution(17328641198469731830)
XLA Ops:
  0.0 0.0 copy-start.1
  0.0 0.0 copy-start
  0.0 0.0 copy-start.2
  0.1 1.4 %collective-permute-start = (f32[24,8,128]{2,1,0:T(8,128)S(1)}, f32[24,8,128]{2,1,0:T(8,128)S(1)}, u32[]{:S(2)}, u32[]{:S(2)}) collective-permute-start(f32[24,8,128]{2,1,0:T(8,128)S(1)} %get-tuple-element.32), channel_id=1, source_target_pairs={{5,4},{9,8},{13,12},{17,16},{21,20},{25,24},{29,28},{33,32},{37,36... | collective-permute-start | bytes 294920 | tf_op jit(solution)/shard_map/ppermute | solution.py:601
  1.5 0.0 copy-done.2
  1.5 0.0 copy-done.1
  1.5 0.0 copy-done
  1.5 0.1 ends.1
  1.6 5.8 %collective-permute-start.1 = (f32[24,8,128]{2,1,0:T(8,128)S(1)}, f32[24,8,128]{2,1,0:T(8,128)S(1)}, u32[]{:S(2)}, u32[]{:S(2)}) collective-permute-start(f32[24,8,128]{2,1,0:T(8,128)S(1)} %get-tuple-element.44), channel_id=1, source_target_pairs={{3,4},{4,3},{5,6},{6,5},{7,8},{8,7},{9,10},{10,9},{11,12},{12,11},... | collective-permute-start | bytes 294920 | tf_op jit(solution)/shard_map/ppermute | solution.py:611
  7.4 0.0 collective-permute-done.one.arrived
  7.5 1.3 %collective-permute-start.2 = (f32[24,8,128]{2,1,0:T(8,128)S(1)}, f32[24,8,128]{2,1,0:T(8,128)S(1)}, u32[]{:S(2)}, u32[]{:S(2)}) collective-permute-start(f32[24,8,128]{2,1,0:T(8,128)S(1)} %third.1), channel_id=1, source_target_pairs={{2,3},{3,2},{6,7},{7,6},{4,5},{10,11},{11,10},{8,9},{14,15},{15,14... | collective-permute-start | bytes 294920 | tf_op jit(solution)/shard_map/ppermute | solution.py:613
  8.8 0.8 %local.1 = (f32[16,3,8,128]{3,2,1,0:T(8,128)S(1)}, f32[2,16,8,128]{3,2,1,0:T(8,128)S(1)}, f32[15,8,8,128]{3,2,1,0:T(8,128)S(1)}, f32[16,3,8,128]{3,2,1,0:T(8,128...) custom-call(f32[3,16,8,128]{3,2,1,0:T(8,128)S(1)} %get-tuple-element, ...), custom_call_target="tpu_custom_call" | custom-call | flops 8388608 | bytes 1048576 | tf_op jit(solution)/shard_map/local/pallas_call | solution.py:556
  9.6 2.8 %collective-permute-done.1.two = f32[24,8,128]{2,1,0:T(8,128)S(1)} collective-permute-done((f32[24,8,128]{2,1,0:T(8,128)S(1)}, f32[24,8,128]{2,1,0:T(8,128)S(1)}, u32[]{:S(2)}, u32[]{:S(2)}) %collective-permute-start.1) | collective-permute-done | bytes 98336 | tf_op jit(solution)/shard_map/ppermute | solution.py:611
  12.4 0.0 collective-permute-done.2.three
  12.4 0.2 %finish.1 = (f32[2,128,128]{2,1,0:T(8,128)S(1)}, f32[8,128]{1,0:T(8,128)S(1)}, f32[16,2,8,128]{3,2,1,0:T(8,128)S(1)}) custom-call(f32[16,3,8,128]{3,2,1,0:T(8,128)S(1)} %get-tuple-element.33.k_all, f32[2,16,8,128]{3,2,1,0:T(8,128)S(1)} %get-tuple-element.34.rhs, f32[3,16,8,128]{3,2,1,0:T(8,128)S(1)} %get-tuple-element.30.kept, ...), custom_call_target="tpu_custom_call" | custom-call | flops 2097152 | bytes 1048576 | tf_op jit(solution)/shard_map/finish/pallas_call | solution.py:556
  12.7 3.2 %all-gather = f32[16,128]{1,0:T(8,128)S(1)} all-gather(f32[8,128]{1,0:T(8,128)S(1)} %get-tuple-element.47), channel_id=2, replica_groups=mesh['line'=2,'tile'=256] {'line'}, dimensions={0}, use_global_device_ids=true | all-gather | bytes 12288 | tf_op jit(solution)/shard_map/all_gather | solution.py:641
  15.9 0.7 %join.1 = f32[2,128,128]{2,1,0:T(8,128)} custom-call(f32[2,128,128]{2,1,0:T(8,128)S(1)} %get-tuple-element.45.local_x, f32[4,128,128]{2,1,0:T(8,128)S(1)} %get-tuple-element.46.answer, f32[2,8,128]{2,1,0:T(8,128)S(1)} %bitcast.1, f32[2,16,8,128]{3,2,1,0:T(8,128)S(1)} %get-tuple-element.34.rhs, f32[16,2,8,128]{3,2,1,0:T(8,128)S(1)} %get-tuple-element.48.pending, ...), custom_call_target="tpu_custom_call" | custom-call | flops 262144 | bytes 1048576 | tf_op jit(solution)/shard_map/join/pallas_call | solution.py:556
  (3 shorter events, 0.1 us)
Async XLA Ops:
  0.0 1.5 %copy-start.1 = (f32[128,128]{1,0:T(8,128)S(1)}, f32[128,128]{1,0:T(8,128)}, u32[]{:S(2)}) copy-start(f32[128,128]{1,0:T(8,128)} %sat.1) | copy-start | bytes 196612
  0.0 1.5 %copy-start = (f32[2,128,128]{2,1,0:T(8,128)S(1)}, f32[2,128,128]{2,1,0:T(8,128)}, u32[]{:S(2)}) copy-start(f32[2,128,128]{2,1,0:T(8,128)} %field.1) | copy-start | bytes 393220
  0.0 1.4 %copy-start.2 = (s32[1,128]{1,0:T(1,128)S(1)}, s32[1,128]{1,0:T(1,128)}, u32[]{:S(2)}) copy-start(s32[1,128]{1,0:T(1,128)} %mask_hbm.1) | copy-start | bytes 1540
  0.1 7.4 %collective-permute-start = (f32[24,8,128]{2,1,0:T(8,128)S(1)}, f32[24,8,128]{2,1,0:T(8,128)S(1)}, u32[]{:S(2)}, u32[]{:S(2)}) collective-permute-start(f32[24,8,128]{2,1,0:T(8,128)S(1)} %get-tuple-element.32), channel_id=1, source_target_pairs={{5,4},{9,8},{13,12},{17,16},{21,20},{25,24},{29,28},{33,32},{37,36... | collective-permute-start | bytes 294920 | tf_op jit(solution)/shard_map/ppermute | solution.py:601
  1.6 10.8 %collective-permute-start.1 = (f32[24,8,128]{2,1,0:T(8,128)S(1)}, f32[24,8,128]{2,1,0:T(8,128)S(1)}, u32[]{:S(2)}, u32[]{:S(2)}) collective-permute-start(f32[24,8,128]{2,1,0:T(8,128)S(1)} %get-tuple-element.44), channel_id=1, source_target_pairs={{3,4},{4,3},{5,6},{6,5},{7,8},{8,7},{9,10},{10,9},{11,12},{12,11},... | collective-permute-start | bytes 294920 | tf_op jit(solution)/shard_map/ppermute | solution.py:611
  7.5 4.9 %collective-permute-start.2 = (f32[24,8,128]{2,1,0:T(8,128)S(1)}, f32[24,8,128]{2,1,0:T(8,128)S(1)}, u32[]{:S(2)}, u32[]{:S(2)}) collective-permute-start(f32[24,8,128]{2,1,0:T(8,128)S(1)} %third.1), channel_id=1, source_target_pairs={{2,3},{3,2},{6,7},{7,6},{4,5},{10,11},{11,10},{8,9},{14,15},{15,14... | collective-permute-start | bytes 294920 | tf_op jit(solution)/shard_map/ppermute | solution.py:613

commit v9 on v8

--- a/solution.py
+++ b/solution.py
@@ -528,8 +528,9 @@
             here = pl.ds(i, CHUNKS, stride=STEPS)
             out[0, here, :] = x[i][0]
             out[1, here, :] = SCALE * x[i][1]
-        for copy in copies:
-            copy.start()
+        whole = pltpu.make_async_copy(out, out_hbm, sems.at[0])
+        whole.start()
+        whole.wait()
 
     @pl.when(line() == 1)
     def _():
@@ -539,9 +540,8 @@
                 change = answer[2 * j, here, :] * through[0] + answer[2 * j + 1, here, :] * through[1]
                 out[j, here, :] = local_x[j, here, :] + change
             copies[j].start()
-
-    for copy in copies:
-        copy.wait()
+        for copy in copies:
+            copy.wait()
 
 
 def tiles(*lead):

time: 16.7 us -> 16.7 us (level)
  no operation moved by 1% of the time
where the time goes in v9:
time: 16.7 us; the launch traced here: 16.6 us
  starting transfers between devices  8.51 us (51%)
  blocking collectives  3.18 us (19%)
  waiting for transfers between devices  2.82 us (17%)
  Pallas kernels  1.95 us (12%)
    ppermute x1, starting transfers between devices, body(): from_two = lax.ppermute(two, both_axes, ops[1])  5.79 us
    all_gather x1, blocking collectives, body(): both = lax.all_gather(message, 'line', axis=0)  3.18 us
    ppermute x1, waiting for transfers between devices, body(): from_two = lax.ppermute(two, both_axes, ops[1])  2.81 us
    pallas_call x7, Pallas kernels, call(): pl.pallas_call(kernel, out_shape=outs, compiler_params=pltpu.CompilerPara...  1.95 us
    ppermute x1, starting transfers between devices, body(): from_one = lax.ppermute(one, both_axes, ops[0])  1.42 us
    ppermute x1, starting transfers between devices, body(): from_three = lax.ppermute(three, both_axes, ops[2])  1.3 us
  transfers between devices with their start and end apart: 3, of which 1 were waited for; matrix products, arithmetic and copies ran while one was open for 0% of the time, Pallas kernels for 6%

profile of v9, /device:TPU:257, one launch (start us, length us, event | category | flops | bytes accessed | tf_op | source)
XLA Modules:
  0.0 16.6 jit_solution(15237675830416795035)
XLA Ops:
  0.0 0.0 copy-start.1
  0.0 0.0 copy-start
  0.0 0.0 copy-start.2
  0.1 1.4 %collective-permute-start = (f32[24,8,128]{2,1,0:T(8,128)S(1)}, f32[24,8,128]{2,1,0:T(8,128)S(1)}, u32[]{:S(2)}, u32[]{:S(2)}) collective-permute-start(f32[24,8,128]{2,1,0:T(8,128)S(1)} %get-tuple-element.32), channel_id=1, source_target_pairs={{5,4},{9,8},{13,12},{17,16},{21,20},{25,24},{29,28},{33,32},{37,36... | collective-permute-start | bytes 294920 | tf_op jit(solution)/shard_map/ppermute | solution.py:601
  1.5 0.0 copy-done.2
  1.5 0.0 copy-done.1
  1.5 0.0 copy-done
  1.5 0.1 ends.1
  1.6 5.8 %collective-permute-start.1 = (f32[24,8,128]{2,1,0:T(8,128)S(1)}, f32[24,8,128]{2,1,0:T(8,128)S(1)}, u32[]{:S(2)}, u32[]{:S(2)}) collective-permute-start(f32[24,8,128]{2,1,0:T(8,128)S(1)} %get-tuple-element.44), channel_id=1, source_target_pairs={{3,4},{4,3},{5,6},{6,5},{7,8},{8,7},{9,10},{10,9},{11,12},{12,11},... | collective-permute-start | bytes 294920 | tf_op jit(solution)/shard_map/ppermute | solution.py:611
  7.4 0.0 collective-permute-done.one.arrived
  7.5 1.3 %collective-permute-start.2 = (f32[24,8,128]{2,1,0:T(8,128)S(1)}, f32[24,8,128]{2,1,0:T(8,128)S(1)}, u32[]{:S(2)}, u32[]{:S(2)}) collective-permute-start(f32[24,8,128]{2,1,0:T(8,128)S(1)} %third.1), channel_id=1, source_target_pairs={{2,3},{3,2},{6,7},{7,6},{4,5},{10,11},{11,10},{8,9},{14,15},{15,14... | collective-permute-start | bytes 294920 | tf_op jit(solution)/shard_map/ppermute | solution.py:613
  8.8 0.8 %local.1 = (f32[16,3,8,128]{3,2,1,0:T(8,128)S(1)}, f32[2,16,8,128]{3,2,1,0:T(8,128)S(1)}, f32[15,8,8,128]{3,2,1,0:T(8,128)S(1)}, f32[16,3,8,128]{3,2,1,0:T(8,128...) custom-call(f32[3,16,8,128]{3,2,1,0:T(8,128)S(1)} %get-tuple-element, ...), custom_call_target="tpu_custom_call" | custom-call | flops 8388608 | bytes 1048576 | tf_op jit(solution)/shard_map/local/pallas_call | solution.py:556
  9.6 2.8 %collective-permute-done.1.two = f32[24,8,128]{2,1,0:T(8,128)S(1)} collective-permute-done((f32[24,8,128]{2,1,0:T(8,128)S(1)}, f32[24,8,128]{2,1,0:T(8,128)S(1)}, u32[]{:S(2)}, u32[]{:S(2)}) %collective-permute-start.1) | collective-permute-done | bytes 98336 | tf_op jit(solution)/shard_map/ppermute | solution.py:611
  12.4 0.0 collective-permute-done.2.three
  12.4 0.2 %finish.1 = (f32[2,128,128]{2,1,0:T(8,128)S(1)}, f32[8,128]{1,0:T(8,128)S(1)}, f32[16,2,8,128]{3,2,1,0:T(8,128)S(1)}) custom-call(f32[16,3,8,128]{3,2,1,0:T(8,128)S(1)} %get-tuple-element.33.k_all, f32[2,16,8,128]{3,2,1,0:T(8,128)S(1)} %get-tuple-element.34.rhs, f32[3,16,8,128]{3,2,1,0:T(8,128)S(1)} %get-tuple-element.30.kept, ...), custom_call_target="tpu_custom_call" | custom-call | flops 2097152 | bytes 1048576 | tf_op jit(solution)/shard_map/finish/pallas_call | solution.py:556
  12.7 3.2 %all-gather = f32[16,128]{1,0:T(8,128)S(1)} all-gather(f32[8,128]{1,0:T(8,128)S(1)} %get-tuple-element.47), channel_id=2, replica_groups=mesh['line'=2,'tile'=256] {'line'}, dimensions={0}, use_global_device_ids=true | all-gather | bytes 12288 | tf_op jit(solution)/shard_map/all_gather | solution.py:641
  15.9 0.7 %join.1 = f32[2,128,128]{2,1,0:T(8,128)} custom-call(f32[2,128,128]{2,1,0:T(8,128)S(1)} %get-tuple-element.45.local_x, f32[4,128,128]{2,1,0:T(8,128)S(1)} %get-tuple-element.46.answer, f32[2,8,128]{2,1,0:T(8,128)S(1)} %bitcast.1, f32[2,16,8,128]{3,2,1,0:T(8,128)S(1)} %get-tuple-element.34.rhs, f32[16,2,8,128]{3,2,1,0:T(8,128)S(1)} %get-tuple-element.48.pending, ...), custom_call_target="tpu_custom_call" | custom-call | flops 262144 | bytes 1048576 | tf_op jit(solution)/shard_map/join/pallas_call | solution.py:556
  (3 shorter events, 0.1 us)
Async XLA Ops:
  0.0 1.5 %copy-start.1 = (f32[128,128]{1,0:T(8,128)S(1)}, f32[128,128]{1,0:T(8,128)}, u32[]{:S(2)}) copy-start(f32[128,128]{1,0:T(8,128)} %sat.1) | copy-start | bytes 196612
  0.0 1.5 %copy-start = (f32[2,128,128]{2,1,0:T(8,128)S(1)}, f32[2,128,128]{2,1,0:T(8,128)}, u32[]{:S(2)}) copy-start(f32[2,128,128]{2,1,0:T(8,128)} %field.1) | copy-start | bytes 393220
  0.0 1.4 %copy-start.2 = (s32[1,128]{1,0:T(1,128)S(1)}, s32[1,128]{1,0:T(1,128)}, u32[]{:S(2)}) copy-start(s32[1,128]{1,0:T(1,128)} %mask_hbm.1) | copy-start | bytes 1540
  0.1 7.4 %collective-permute-start = (f32[24,8,128]{2,1,0:T(8,128)S(1)}, f32[24,8,128]{2,1,0:T(8,128)S(1)}, u32[]{:S(2)}, u32[]{:S(2)}) collective-permute-start(f32[24,8,128]{2,1,0:T(8,128)S(1)} %get-tuple-element.32), channel_id=1, source_target_pairs={{5,4},{9,8},{13,12},{17,16},{21,20},{25,24},{29,28},{33,32},{37,36... | collective-permute-start | bytes 294920 | tf_op jit(solution)/shard_map/ppermute | solution.py:601
  1.6 10.8 %collective-permute-start.1 = (f32[24,8,128]{2,1,0:T(8,128)S(1)}, f32[24,8,128]{2,1,0:T(8,128)S(1)}, u32[]{:S(2)}, u32[]{:S(2)}) collective-permute-start(f32[24,8,128]{2,1,0:T(8,128)S(1)} %get-tuple-element.44), channel_id=1, source_target_pairs={{3,4},{4,3},{5,6},{6,5},{7,8},{8,7},{9,10},{10,9},{11,12},{12,11},... | collective-permute-start | bytes 294920 | tf_op jit(solution)/shard_map/ppermute | solution.py:611
  7.5 4.9 %collective-permute-start.2 = (f32[24,8,128]{2,1,0:T(8,128)S(1)}, f32[24,8,128]{2,1,0:T(8,128)S(1)}, u32[]{:S(2)}, u32[]{:S(2)}) collective-permute-start(f32[24,8,128]{2,1,0:T(8,128)S(1)} %third.1), channel_id=1, source_target_pairs={{2,3},{3,2},{6,7},{7,6},{4,5},{10,11},{11,10},{8,9},{14,15},{15,14... | collective-permute-start | bytes 294920 | tf_op jit(solution)/shard_map/ppermute | solution.py:613

commit v10 on v9

--- a/solution.py
+++ b/solution.py
@@ -387,16 +387,16 @@
 
         @pl.when(line() == 0)
         def _():
+            message[...] = share[...]
+            for i in range(half):
+                store(pending, (i,), through[i])
             parts = [apply(turn(load(own_green, i)), through[i]) for i in range(half)]
             while len(parts) > 1:
                 parts = [add(x, y) for x, y in zip(parts[::2], parts[1::2])]
             d = over_chunks(parts[0])
-            message[...] = share[...]
             for j in range(2):
                 x = known[j] + jnp.where(near, d[j] + roll(d[j], XS, 1), 0.0)
                 message[pl.ds(j, 1), :] = x[0:1]
-            for i in range(half):
-                store(pending, (i,), through[i])
 
         @pl.when(line() == 1)
         def _():

time: 16.7 us -> 16.7 us (level)
  no operation moved by 1% of the time
where the time goes in v10:
time: 16.7 us; the launch traced here: 16.6 us
  starting transfers between devices  8.51 us (51%)
  blocking collectives  3.18 us (19%)
  waiting for transfers between devices  2.82 us (17%)
  Pallas kernels  1.95 us (12%)
    ppermute x1, starting transfers between devices, body(): from_two = lax.ppermute(two, both_axes, ops[1])  5.79 us
    all_gather x1, blocking collectives, body(): both = lax.all_gather(message, 'line', axis=0)  3.18 us
    ppermute x1, waiting for transfers between devices, body(): from_two = lax.ppermute(two, both_axes, ops[1])  2.81 us
    pallas_call x7, Pallas kernels, call(): pl.pallas_call(kernel, out_shape=outs, compiler_params=pltpu.CompilerPara...  1.95 us
    ppermute x1, starting transfers between devices, body(): from_one = lax.ppermute(one, both_axes, ops[0])  1.42 us
    ppermute x1, starting transfers between devices, body(): from_three = lax.ppermute(three, both_axes, ops[2])  1.3 us
  transfers between devices with their start and end apart: 3, of which 1 were waited for; matrix products, arithmetic and copies ran while one was open for 0% of the time, Pallas kernels for 6%

profile of v10, /device:TPU:257, one launch (start us, length us, event | category | flops | bytes accessed | tf_op | source)
XLA Modules:
  0.0 16.6 jit_solution(16931917275318146097)
XLA Ops:
  0.0 0.0 copy-start.1
  0.0 0.0 copy-start
  0.0 0.0 copy-start.2
  0.1 1.4 %collective-permute-start = (f32[24,8,128]{2,1,0:T(8,128)S(1)}, f32[24,8,128]{2,1,0:T(8,128)S(1)}, u32[]{:S(2)}, u32[]{:S(2)}) collective-permute-start(f32[24,8,128]{2,1,0:T(8,128)S(1)} %get-tuple-element.32), channel_id=1, source_target_pairs={{5,4},{9,8},{13,12},{17,16},{21,20},{25,24},{29,28},{33,32},{37,36... | collective-permute-start | bytes 294920 | tf_op jit(solution)/shard_map/ppermute | solution.py:601
  1.5 0.0 copy-done.2
  1.5 0.0 copy-done.1
  1.5 0.0 copy-done
  1.5 0.1 ends.1
  1.6 5.8 %collective-permute-start.1 = (f32[24,8,128]{2,1,0:T(8,128)S(1)}, f32[24,8,128]{2,1,0:T(8,128)S(1)}, u32[]{:S(2)}, u32[]{:S(2)}) collective-permute-start(f32[24,8,128]{2,1,0:T(8,128)S(1)} %get-tuple-element.44), channel_id=1, source_target_pairs={{3,4},{4,3},{5,6},{6,5},{7,8},{8,7},{9,10},{10,9},{11,12},{12,11},... | collective-permute-start | bytes 294920 | tf_op jit(solution)/shard_map/ppermute | solution.py:611
  7.4 0.0 collective-permute-done.one.arrived
  7.5 1.3 %collective-permute-start.2 = (f32[24,8,128]{2,1,0:T(8,128)S(1)}, f32[24,8,128]{2,1,0:T(8,128)S(1)}, u32[]{:S(2)}, u32[]{:S(2)}) collective-permute-start(f32[24,8,128]{2,1,0:T(8,128)S(1)} %third.1), channel_id=1, source_target_pairs={{2,3},{3,2},{6,7},{7,6},{4,5},{10,11},{11,10},{8,9},{14,15},{15,14... | collective-permute-start | bytes 294920 | tf_op jit(solution)/shard_map/ppermute | solution.py:613
  8.8 0.8 %local.1 = (f32[16,3,8,128]{3,2,1,0:T(8,128)S(1)}, f32[2,16,8,128]{3,2,1,0:T(8,128)S(1)}, f32[15,8,8,128]{3,2,1,0:T(8,128)S(1)}, f32[16,3,8,128]{3,2,1,0:T(8,128...) custom-call(f32[3,16,8,128]{3,2,1,0:T(8,128)S(1)} %get-tuple-element, ...), custom_call_target="tpu_custom_call" | custom-call | flops 8388608 | bytes 1048576 | tf_op jit(solution)/shard_map/local/pallas_call | solution.py:556
  9.6 2.8 %collective-permute-done.1.two = f32[24,8,128]{2,1,0:T(8,128)S(1)} collective-permute-done((f32[24,8,128]{2,1,0:T(8,128)S(1)}, f32[24,8,128]{2,1,0:T(8,128)S(1)}, u32[]{:S(2)}, u32[]{:S(2)}) %collective-permute-start.1) | collective-permute-done | bytes 98336 | tf_op jit(solution)/shard_map/ppermute | solution.py:611
  12.4 0.0 collective-permute-done.2.three
  12.4 0.2 %finish.1 = (f32[2,128,128]{2,1,0:T(8,128)S(1)}, f32[8,128]{1,0:T(8,128)S(1)}, f32[16,2,8,128]{3,2,1,0:T(8,128)S(1)}) custom-call(f32[16,3,8,128]{3,2,1,0:T(8,128)S(1)} %get-tuple-element.33.k_all, f32[2,16,8,128]{3,2,1,0:T(8,128)S(1)} %get-tuple-element.34.rhs, f32[3,16,8,128]{3,2,1,0:T(8,128)S(1)} %get-tuple-element.30.kept, ...), custom_call_target="tpu_custom_call" | custom-call | flops 2097152 | bytes 1048576 | tf_op jit(solution)/shard_map/finish/pallas_call | solution.py:556
  12.7 3.2 %all-gather = f32[16,128]{1,0:T(8,128)S(1)} all-gather(f32[8,128]{1,0:T(8,128)S(1)} %get-tuple-element.47), channel_id=2, replica_groups=mesh['line'=2,'tile'=256] {'line'}, dimensions={0}, use_global_device_ids=true | all-gather | bytes 12288 | tf_op jit(solution)/shard_map/all_gather | solution.py:641
  15.9 0.7 %join.1 = f32[2,128,128]{2,1,0:T(8,128)} custom-call(f32[2,128,128]{2,1,0:T(8,128)S(1)} %get-tuple-element.45.local_x, f32[4,128,128]{2,1,0:T(8,128)S(1)} %get-tuple-element.46.answer, f32[2,8,128]{2,1,0:T(8,128)S(1)} %bitcast.1, f32[2,16,8,128]{3,2,1,0:T(8,128)S(1)} %get-tuple-element.34.rhs, f32[16,2,8,128]{3,2,1,0:T(8,128)S(1)} %get-tuple-element.48.pending, ...), custom_call_target="tpu_custom_call" | custom-call | flops 262144 | bytes 1048576 | tf_op jit(solution)/shard_map/join/pallas_call | solution.py:556
  (3 shorter events, 0.1 us)
Async XLA Ops:
  0.0 1.5 %copy-start.1 = (f32[128,128]{1,0:T(8,128)S(1)}, f32[128,128]{1,0:T(8,128)}, u32[]{:S(2)}) copy-start(f32[128,128]{1,0:T(8,128)} %sat.1) | copy-start | bytes 196612
  0.0 1.5 %copy-start = (f32[2,128,128]{2,1,0:T(8,128)S(1)}, f32[2,128,128]{2,1,0:T(8,128)}, u32[]{:S(2)}) copy-start(f32[2,128,128]{2,1,0:T(8,128)} %field.1) | copy-start | bytes 393220
  0.0 1.4 %copy-start.2 = (s32[1,128]{1,0:T(1,128)S(1)}, s32[1,128]{1,0:T(1,128)}, u32[]{:S(2)}) copy-start(s32[1,128]{1,0:T(1,128)} %mask_hbm.1) | copy-start | bytes 1540
  0.1 7.4 %collective-permute-start = (f32[24,8,128]{2,1,0:T(8,128)S(1)}, f32[24,8,128]{2,1,0:T(8,128)S(1)}, u32[]{:S(2)}, u32[]{:S(2)}) collective-permute-start(f32[24,8,128]{2,1,0:T(8,128)S(1)} %get-tuple-element.32), channel_id=1, source_target_pairs={{5,4},{9,8},{13,12},{17,16},{21,20},{25,24},{29,28},{33,32},{37,36... | collective-permute-start | bytes 294920 | tf_op jit(solution)/shard_map/ppermute | solution.py:601
  1.6 10.8 %collective-permute-start.1 = (f32[24,8,128]{2,1,0:T(8,128)S(1)}, f32[24,8,128]{2,1,0:T(8,128)S(1)}, u32[]{:S(2)}, u32[]{:S(2)}) collective-permute-start(f32[24,8,128]{2,1,0:T(8,128)S(1)} %get-tuple-element.44), channel_id=1, source_target_pairs={{3,4},{4,3},{5,6},{6,5},{7,8},{8,7},{9,10},{10,9},{11,12},{12,11},... | collective-permute-start | bytes 294920 | tf_op jit(solution)/shard_map/ppermute | solution.py:611
  7.5 4.9 %collective-permute-start.2 = (f32[24,8,128]{2,1,0:T(8,128)S(1)}, f32[24,8,128]{2,1,0:T(8,128)S(1)}, u32[]{:S(2)}, u32[]{:S(2)}) collective-permute-start(f32[24,8,128]{2,1,0:T(8,128)S(1)} %third.1), channel_id=1, source_target_pairs={{2,3},{3,2},{6,7},{7,6},{4,5},{10,11},{11,10},{8,9},{14,15},{15,14... | collective-permute-start | bytes 294920 | tf_op jit(solution)/shard_map/ppermute | solution.py:613
